TPU v7x, 256 devices: a whole 4x4x8 slice. The times are simulated.
256 devices in a mesh: seq: 64 (over y, z, core), chan: 4 (over x).
Axes of the slice: x: 4, y: 4, z: 8, core: 2. Of those that a mesh axis runs over, the one named last changes fastest.
Arguments:
- query_proj: bfloat16 [16384, 4096], P('seq', 'chan'), may hold values from -6 to 6
- key_proj: bfloat16 [16384, 4096], P('seq', 'chan'), may hold values from -6 to 6
- value_proj: bfloat16 [16384, 4096], P('seq', 'chan'), may hold values from -6 to 6
- out_grad: bfloat16 [16384, 4096], P('seq', 'chan'), may hold values from -6 to 6
- residues: float32 [256, 16], replicated, may hold values from -2.1 to 2.1
- decay_rate: float32 [256, 16], replicated, as said below
- skip_gain: float32 [4096], P('chan'), may hold values from -3 to 3
Outputs:
- layer_out: bfloat16 [16384, 4096], P('seq', 'chan')
- key_grad: bfloat16 [16384, 4096], P('seq', 'chan')
- value_grad: bfloat16 [16384, 4096], P('seq', 'chan')
- filter_grad: float32 [16384, 256], P('seq', 'chan')
Inputs may be any that keep to these rules, and one draw needn't show every extreme that they name: `decay_rate`: every rate is positive.
All inputs are finite; a program needn't handle non-finite values.
Results may differ from a plain program's by a relative error of at most 0.022.
Values may be sent and summed in bfloat16 or wider, within the bound.
A program may use at most 192 MiB of HBM per device.

v0:
```python
import math

import jax
import jax.numpy as jnp
from jax import lax
from jax.sharding import PartitionSpec as P

CHANNELS = 4096
FILTERS = 256


PRECISE = lax.Precision.HIGHEST


def for_sending(shard):
    return jax.tree.map(lambda a: a.astype(jnp.bfloat16) if a.dtype == jnp.float32 else a, shard)


def partner(block, axis, apart):
    count = lax.axis_size(axis)
    route = []
    for low in range(count):
        high = low | 1 << apart
        if high != low and high < count:
            route += [(low, high), (high, low)]
    return lax.ppermute(block, axis, route)


def phase_pair(exponent, period, direction):
    angles = 2.0 * math.pi / period * exponent.astype(jnp.float32)
    return (jnp.cos(angles), direction * jnp.sin(angles))


def dft_matrix(order_size, direction):
    counter = jnp.arange(order_size, dtype=jnp.int32)
    exponent = counter[:, None] * counter[None, :] % order_size
    return phase_pair(exponent, order_size, direction)


def complex_mix(matrix, values_re, values_im, pattern):
    matrix_re, matrix_im = matrix
    out_re = jnp.einsum(pattern, matrix_re, values_re, precision=PRECISE) - jnp.einsum(
        pattern, matrix_im, values_im, precision=PRECISE
    )
    out_im = jnp.einsum(pattern, matrix_re, values_im, precision=PRECISE) + jnp.einsum(
        pattern, matrix_im, values_re, precision=PRECISE
    )
    return (out_re, out_im)


def complex_times(first_re, first_im, second_re, second_im):
    return (
        first_re * second_re - first_im * second_im,
        first_re * second_im + first_im * second_re,
    )


def split_halves(signal_re, signal_im, turn_re, turn_im):
    odd_re, odd_im = complex_times(signal_re, signal_im, turn_re, turn_im)
    return (jnp.stack([signal_re, odd_re]), jnp.stack([signal_im, odd_im]))


def join_halves(halves_re, halves_im, turn_re, turn_im, factor):
    back_re, back_im = complex_times(halves_re[1], halves_im[1], turn_re, -turn_im)
    return ((halves_re[0] + back_re) * factor, (halves_im[0] + back_im) * factor)


def filter_rows(residues, decay_rate, places):
    weight = residues * jnp.sqrt(decay_rate)
    decays = jnp.exp(-(decay_rate[:, :, None] * places[None, None, :]))
    return jnp.sum(weight[:, :, None] * decays, axis=1)


def block_turn(seq_index, shards, tok_rows, direction):
    slab_rows = tok_rows // shards
    orders = jnp.arange(shards, dtype=jnp.int32)[:, None]
    offsets = seq_index * slab_rows + jnp.arange(slab_rows, dtype=jnp.int32)[None, :]
    return phase_pair(orders * offsets % (shards * tok_rows), shards * tok_rows, direction)


def spread_forward(signal_re, signal_im, first_matrix, last_matrix, turn):
    halves, tok_rows, col_count = signal_re.shape
    shards = lax.axis_size("seq")
    signal_re = signal_re.reshape(halves, shards, tok_rows // shards, col_count)
    signal_im = signal_im.reshape(halves, shards, tok_rows // shards, col_count)

    def across(pieces):
        mixed_re, mixed_im = complex_mix(first_matrix, pieces[0], pieces[1], "kp,eprc->ekrc")
        return complex_times(
            mixed_re, mixed_im, turn[0][None, :, :, None], turn[1][None, :, :, None]
        )

    cross_re, cross_im = across(
        (
            lax.all_to_all(
                signal_re.astype(jnp.bfloat16), "seq", split_axis=1, concat_axis=1, tiled=True
            ).astype(signal_re.dtype),
            lax.all_to_all(
                signal_im.astype(jnp.bfloat16), "seq", split_axis=1, concat_axis=1, tiled=True
            ).astype(signal_im.dtype),
        )
    )
    spec_re, spec_im = (
        lax.all_to_all(
            for_sending(cross_re), "seq", split_axis=1, concat_axis=2, tiled=True
        ).astype(cross_re.dtype),
        lax.all_to_all(
            for_sending(cross_im), "seq", split_axis=1, concat_axis=2, tiled=True
        ).astype(cross_im.dtype),
    )
    spec_re = spec_re.reshape(halves, tok_rows, col_count)
    spec_im = spec_im.reshape(halves, tok_rows, col_count)
    return complex_mix(last_matrix, spec_re, spec_im, "kj,ejc->ekc")


def spread_inverse(spec_re, spec_im, first_matrix, last_matrix, turn):
    halves, tok_rows, col_count = spec_re.shape
    rows_re, rows_im = complex_mix(last_matrix, spec_re, spec_im, "jk,ekc->ejc")
    rows_re = rows_re.reshape(halves, 1, tok_rows, col_count)
    rows_im = rows_im.reshape(halves, 1, tok_rows, col_count)

    def across(pieces):
        turned_re, turned_im = complex_times(
            pieces[0], pieces[1], turn[0][None, :, :, None], turn[1][None, :, :, None]
        )
        return complex_mix(first_matrix, turned_re, turned_im, "pk,ekrc->eprc")

    cross_re, cross_im = across(
        (
            lax.all_to_all(
                for_sending(rows_re), "seq", split_axis=2, concat_axis=1, tiled=True
            ).astype(rows_re.dtype),
            lax.all_to_all(
                for_sending(rows_im), "seq", split_axis=2, concat_axis=1, tiled=True
            ).astype(rows_im.dtype),
        )
    )
    back_re, back_im = (
        lax.all_to_all(
            for_sending(cross_re), "seq", split_axis=1, concat_axis=2, tiled=True
        ).astype(cross_re.dtype),
        lax.all_to_all(
            for_sending(cross_im), "seq", split_axis=1, concat_axis=2, tiled=True
        ).astype(cross_im.dtype),
    )
    return (
        back_re.reshape(halves, tok_rows, col_count),
        back_im.reshape(halves, tok_rows, col_count),
    )


def butterfly_spectrum(residues, decay_rate, seq_index, shards, tok_rows, last_matrix):
    length = shards * tok_rows
    levels = shards.bit_length() - 1
    mirror = jnp.zeros((), jnp.int32)
    for level_bit in range(levels):
        digit_bit = jnp.bitwise_and(jnp.right_shift(seq_index, level_bit), 1)
        mirror = mirror + jnp.left_shift(digit_bit, levels - 1 - level_bit)
    places_int = mirror * tok_rows + jnp.arange(tok_rows, dtype=jnp.int32)
    taps_now = filter_rows(residues, decay_rate, places_int.astype(jnp.float32)).T
    turn_re, turn_im = phase_pair(places_int, 2 * length, -1.0)
    state_re, state_im = split_halves(
        taps_now, jnp.zeros_like(taps_now), turn_re[:, None], turn_im[:, None]
    )
    for level_bit in range(levels):
        other_re, other_im = (
            partner(state_re.astype(jnp.bfloat16), "seq", level_bit).astype(state_re.dtype),
            partner(state_im.astype(jnp.bfloat16), "seq", level_bit).astype(state_im.dtype),
        )
        upper_half = jnp.bitwise_and(jnp.right_shift(seq_index, level_bit), 1) == 1
        offset = jnp.bitwise_and(seq_index, (1 << level_bit) - 1)
        factor_re, factor_im = phase_pair(offset, 2 << level_bit, -1.0)
        base_re = jnp.where(upper_half, other_re, state_re)
        base_im = jnp.where(upper_half, other_im, state_im)
        tail_re = jnp.where(upper_half, state_re, other_re)
        tail_im = jnp.where(upper_half, state_im, other_im)
        sign_flip = jnp.where(upper_half, -1.0, 1.0)
        prod_re, prod_im = complex_times(tail_re, tail_im, factor_re, factor_im)
        state_re = base_re + sign_flip * prod_re
        state_im = base_im + sign_flip * prod_im
    final_re, final_im = phase_pair(
        seq_index * jnp.arange(tok_rows, dtype=jnp.int32) % length, length, -1.0
    )
    state_re, state_im = complex_times(
        state_re, state_im, final_re[None, :, None], final_im[None, :, None]
    )
    return complex_mix(last_matrix, state_re, state_im, "kj,ejc->ekc")


def sequence_layout(conv_wide, grad_wide, residues, decay_rate, matrices):
    fwd_first, fwd_last, inv_first, inv_last = matrices
    shards = lax.axis_size("seq")
    seq_index = lax.axis_index("seq")
    tok_rows, chan_width = conv_wide.shape
    pair_count = chan_width // 2
    length = shards * tok_rows
    places_int = seq_index * tok_rows + jnp.arange(tok_rows, dtype=jnp.int32)
    turn_re, turn_im = phase_pair(places_int, 2 * length, -1.0)
    signal_re = jnp.concatenate([conv_wide[:, :pair_count], grad_wide[:, :pair_count]], axis=1)
    signal_im = jnp.concatenate([conv_wide[:, pair_count:], grad_wide[:, pair_count:]], axis=1)
    halves_re, halves_im = split_halves(signal_re, signal_im, turn_re[:, None], turn_im[:, None])
    fwd_turn = block_turn(seq_index, shards, tok_rows, -1.0)
    spec_re, spec_im = spread_forward(halves_re, halves_im, fwd_first, fwd_last, fwd_turn)
    filt_re, filt_im = butterfly_spectrum(
        residues, decay_rate, seq_index, shards, tok_rows, fwd_last
    )
    repeats = pair_count // FILTERS
    filt_re = jnp.tile(filt_re, (1, 1, repeats))
    filt_im = jnp.tile(filt_im, (1, 1, repeats))
    head_re = spec_re[:, :, :pair_count]
    head_im = spec_im[:, :, :pair_count]
    tail_re = spec_re[:, :, pair_count:chan_width]
    tail_im = spec_im[:, :, pair_count:chan_width]
    conv_re, conv_im = complex_times(filt_re, filt_im, head_re, head_im)
    corr_re, corr_im = complex_times(filt_re, -filt_im, tail_re, tail_im)
    cross_re, cross_im = complex_times(tail_re, tail_im, head_re, -head_im)
    cross_re = cross_re.reshape(2, tok_rows, repeats, FILTERS).sum(axis=2)
    cross_im = cross_im.reshape(2, tok_rows, repeats, FILTERS).sum(axis=2)
    share_re, share_im = (
        lax.psum_scatter(
            cross_re.astype(jnp.bfloat16), "chan", scatter_dimension=2, tiled=True
        ).astype(jnp.float32),
        lax.psum_scatter(
            cross_im.astype(jnp.bfloat16), "chan", scatter_dimension=2, tiled=True
        ).astype(jnp.float32),
    )
    inv_turn = block_turn(seq_index, shards, tok_rows, 1.0)
    back_re, back_im = spread_inverse(
        jnp.concatenate([conv_re, corr_re, share_re], axis=2),
        jnp.concatenate([conv_im, corr_im, share_im], axis=2),
        inv_first,
        inv_last,
        inv_turn,
    )
    value_re, value_im = join_halves(
        back_re, back_im, turn_re[:, None], turn_im[:, None], 1.0 / (2 * length)
    )
    conv_out = jnp.concatenate([value_re[:, :pair_count], value_im[:, :pair_count]], axis=1)
    corr_out = jnp.concatenate(
        [value_re[:, pair_count:chan_width], value_im[:, pair_count:chan_width]], axis=1
    )
    return (conv_out, corr_out, value_re[:, chan_width:])


def per_device(query_proj, key_proj, value_proj, out_grad, residues, decay_rate, skip_gain):
    tok_rows = key_proj.shape[0]
    shards = lax.axis_size("seq")
    length = shards * tok_rows
    matrices = (
        dft_matrix(shards, -1.0),
        dft_matrix(tok_rows, -1.0),
        dft_matrix(shards, 1.0),
        dft_matrix(tok_rows, 1.0),
    )
    conv_in = (key_proj.astype(jnp.float32) * value_proj.astype(jnp.float32)).astype(jnp.bfloat16)
    mid_grad = (out_grad.astype(jnp.float32) * query_proj.astype(jnp.float32)).astype(jnp.bfloat16)
    conv_wide = conv_in.astype(jnp.float32)
    grad_wide = mid_grad.astype(jnp.float32)
    conv_out, corr_out, taps_grad = sequence_layout(
        conv_wide, grad_wide, residues, decay_rate, matrices
    )
    gain_row = skip_gain[None, :]
    layer_out = (query_proj.astype(jnp.float32) * (conv_out + gain_row * conv_wide)).astype(
        jnp.bfloat16
    )
    total_grad = corr_out + gain_row * grad_wide
    key_grad = (total_grad * value_proj.astype(jnp.float32)).astype(jnp.bfloat16)
    value_grad = (total_grad * key_proj.astype(jnp.float32)).astype(jnp.bfloat16)
    filter_grad = taps_grad * (1.0 / math.sqrt(length * (CHANNELS // FILTERS)))
    return (layer_out, key_grad, value_grad, filter_grad)


def solution(mesh):
    placed = (
        P("seq", "chan"),
        P("seq", "chan"),
        P("seq", "chan"),
        P("seq", "chan"),
        P(),
        P(),
        P("chan"),
    )
    return jax.shard_map(
        per_device,
        mesh=mesh,
        in_specs=placed,
        out_specs=(P("seq", "chan"), P("seq", "chan"), P("seq", "chan"), P("seq", "chan")),
        check_vma=False,
    )
```

profile of v0, /device:TPU:1, one launch (start us, length us, event | category | flops | bytes accessed | tf_op | source)
XLA Modules:
  0.0 527.1 jit_solution(13828243137242337314)
XLA Ops:
  14.3 2.0 pad_maximum_fusion.9
  16.3 2.0 stack.34
  22.9 13.2 %all-to-all-start = ((bf16[2,64,4,1024]{3,2,0,1:T(4,128)(2,1)}), bf16[2,64,4,1024]{3,2,0,1:T(4,128)(2,1)S(1)}, u32[]{:S(2)}, u32[]{:S(2)}) async-start(bf16[2,64,4,1024]{3,2,0,1:T(4,128)(2,1)} %copy.84), calls=%async_computation | async-start | bytes 2097152 | tf_op jit(solution)/shard_map/all_to_all | solution.py:95
  38.6 26.0 %all-to-all-done = bf16[2,64,4,1024]{3,2,0,1:T(4,128)(2,1)S(1)} async-done(((bf16[2,64,4,1024]{3,2,0,1:T(4,128)(2,1)}), bf16[2,64,4,1024]{3,2,0,1:T(4,128)(2,1)S(1)}, u32[]{:S(2)}, u32[]{:S(2)}) %all-to-all-start) | async-done | bytes 1048608 | tf_op jit(solution)/shard_map/all_to_all | solution.py:95
  64.6 6.2 %all-to-all-start.1 = ((bf16[2,64,4,1024]{3,2,0,1:T(4,128)(2,1)}), bf16[2,64,4,1024]{3,2,0,1:T(4,128)(2,1)S(1)}, u32[]{:S(2)}, u32[]{:S(2)}) async-start(bf16[2,64,4,1024]{3,2,0,1:T(4,128)(2,1)} %copy.86), calls=%async_computation.1 | async-start | bytes 2097152 | tf_op jit(solution)/shard_map/all_to_all | solution.py:98
  71.2 2.9 multiply_reduce_fusion
  75.5 3.1 fusion.39
  78.5 20.8 %all-to-all-done.1 = bf16[2,64,4,1024]{3,2,0,1:T(4,128)(2,1)S(1)} async-done(((bf16[2,64,4,1024]{3,2,0,1:T(4,128)(2,1)}), bf16[2,64,4,1024]{3,2,0,1:T(4,128)(2,1)S(1)}, u32[]{:S(2)}, u32[]{:S(2)}) %all-to-all-start.1) | async-done | bytes 1048608 | tf_op jit(solution)/shard_map/all_to_all | solution.py:98
  102.9 2.4 fusion.17
  107.2 6.2 %all-to-all-start.2 = ((bf16[2,64,4,1024]{3,2,0,1:T(4,128)(2,1)}), bf16[2,64,4,1024]{3,2,0,1:T(4,128)(2,1)S(1)}, u32[]{:S(2)}, u32[]{:S(2)}) async-start(bf16[2,64,4,1024]{3,2,0,1:T(4,128)(2,1)} %copy.90), calls=%async_computation.2 | async-start | bytes 2097152 | tf_op jit(solution)/shard_map/all_to_all | solution.py:104
  113.4 2.3 fusion.251
  117.3 26.2 %collective-permute-done.2 = bf16[2,256,256]{1,2,0:T(8,128)(2,1)S(1)} collective-permute-done((bf16[2,256,256]{1,2,0:T(8,128)(2,1)S(1)}, bf16[2,256,256]{1,2,0:T(8,128)(2,1)S(1)}, u32[]{:S(2)}, u32[]{:S(2)}) %collective-permute-start.2) | collective-permute-done | bytes 262176 | tf_op jit(solution)/shard_map/ppermute | solution.py:26
  143.4 5.6 %collective-permute-done.3 = bf16[2,256,256]{1,2,0:T(8,128)(2,1)S(1)} collective-permute-done((bf16[2,256,256]{1,2,0:T(8,128)(2,1)S(1)}, bf16[2,256,256]{1,2,0:T(8,128)(2,1)S(1)}, u32[]{:S(2)}, u32[]{:S(2)}) %collective-permute-start.3) | collective-permute-done | bytes 262176 | tf_op jit(solution)/shard_map/ppermute | solution.py:26
  149.8 2.3 fusion.247
  152.1 2.1 collective-permute-start.4
  154.6 18.0 %collective-permute-done.4 = bf16[2,256,256]{1,2,0:T(8,128)(2,1)} collective-permute-done((bf16[2,256,256]{1,2,0:T(8,128)(2,1)}, bf16[2,256,256]{1,2,0:T(8,128)(2,1)}, u32[]{:S(2)}, u32[]{:S(2)}) %collective-permute-start.4) | collective-permute-done | bytes 262176 | tf_op jit(solution)/shard_map/ppermute | solution.py:26
  172.6 5.6 %collective-permute-done.5 = bf16[2,256,256]{1,2,0:T(8,128)(2,1)} collective-permute-done((bf16[2,256,256]{1,2,0:T(8,128)(2,1)S(1)}, bf16[2,256,256]{1,2,0:T(8,128)(2,1)}, u32[]{:S(2)}, u32[]{:S(2)}) %collective-permute-start.5) | collective-permute-done | bytes 262176 | tf_op jit(solution)/shard_map/ppermute | solution.py:26
  178.2 2.3 fusion.243
  180.5 3.7 collective-permute-start.6
  184.2 1.8 collective-permute-start.7
  186.2 17.7 %collective-permute-done.6 = bf16[2,256,256]{1,2,0:T(8,128)(2,1)S(1)} collective-permute-done((bf16[2,256,256]{1,2,0:T(8,128)(2,1)}, bf16[2,256,256]{1,2,0:T(8,128)(2,1)S(1)}, u32[]{:S(2)}, u32[]{:S(2)}) %collective-permute-start.6) | collective-permute-done | bytes 262176 | tf_op jit(solution)/shard_map/ppermute | solution.py:26
  204.0 5.6 %collective-permute-done.7 = bf16[2,256,256]{1,2,0:T(8,128)(2,1)S(1)} collective-permute-done((bf16[2,256,256]{1,2,0:T(8,128)(2,1)S(1)}, bf16[2,256,256]{1,2,0:T(8,128)(2,1)S(1)}, u32[]{:S(2)}, u32[]{:S(2)}) %collective-permute-start.7) | collective-permute-done | bytes 262176 | tf_op jit(solution)/shard_map/ppermute | solution.py:26
  210.3 2.3 fusion.239
  216.0 8.3 %all-to-all-start.3 = ((bf16[2,64,4,1024]{3,2,0,1:T(4,128)(2,1)}), bf16[2,64,4,1024]{3,2,0,1:T(4,128)(2,1)S(1)}, u32[]{:S(2)}, u32[]{:S(2)}) async-start(bf16[2,64,4,1024]{3,2,0,1:T(4,128)(2,1)} %copy.93), calls=%async_computation.3 | async-start | bytes 2097152 | tf_op jit(solution)/shard_map/all_to_all | solution.py:107
  225.6 2.3 fusion.235
  227.9 3.0 collective-permute-start.10
  231.3 10.1 %collective-permute-done.10 = bf16[2,256,256]{1,2,0:T(8,128)(2,1)S(1)} collective-permute-done((bf16[2,256,256]{1,2,0:T(8,128)(2,1)}, bf16[2,256,256]{1,2,0:T(8,128)(2,1)S(1)}, u32[]{:S(2)}, u32[]{:S(2)}) %collective-permute-start.10) | collective-permute-done | bytes 262176 | tf_op jit(solution)/shard_map/ppermute | solution.py:26
  241.3 10.6 %collective-permute-done.11 = bf16[2,256,256]{1,2,0:T(8,128)(2,1)S(1)} collective-permute-done((bf16[2,256,256]{1,2,0:T(8,128)(2,1)S(1)}, bf16[2,256,256]{1,2,0:T(8,128)(2,1)S(1)}, u32[]{:S(2)}, u32[]{:S(2)}) %collective-permute-start.11) | collective-permute-done | bytes 262176 | tf_op jit(solution)/shard_map/ppermute | solution.py:26
  256.5 2.4 fusion.25
  258.9 2.4 fusion.24
  263.7 3.3 fusion.71
  269.2 2.0 fusion.67
  271.2 2.0 subtract_bitcast_fusion
  273.3 2.0 add_bitcast_fusion
  275.3 2.4 fusion.34
  277.7 2.1 reduce_sum.29
  280.3 2.1 reduce_sum.28
  282.4 18.4 %reduce-scatter.5.cloned.1.call-done = bf16[2,256,64]{1,2,0:T(8,128)(2,1)} async-done(((bf16[2,256,256]{1,2,0:T(8,128)(2,1)}), bf16[2,256,64]{1,2,0:T(8,128)(2,1)}) %reduce-scatter.5.cloned.1.call-update) | async-done | bytes 65552 | tf_op jit(solution)/shard_map/reduce_scatter | solution.py:223
  301.7 4.2 fusion.20
  305.9 21.1 %reduce-scatter.3.cloned.1.call-done = bf16[2,256,64]{1,2,0:T(8,128)(2,1)} async-done(((bf16[2,256,256]{1,2,0:T(8,128)(2,1)}), bf16[2,256,64]{1,2,0:T(8,128)(2,1)}) %reduce-scatter.3.cloned.1.call-update) | async-done | bytes 65552 | tf_op jit(solution)/shard_map/reduce_scatter | solution.py:220
  327.9 5.8 %fusion.4 = bf16[2,1,256,1088]{2,3,0,1:T(8,128)(2,1)} fusion(f32[2,1088,256]{2,1,0:T(8,128)} %fusion.20, f32[2,256,64]{1,2,0:T(8,128)S(1)} %convert_element_type.358, f32[2,256,512]{1,2,0:T(8,128)S(1)} %get-tuple-element.42, f32[2,256,512]{1,2,0:T(8,128)} %get-tuple-element.43), kind=kOutput, calls=%fused_computation.13 | convolution fusion | flops 1714421760 | bytes 5570560 | tf_op jit(solution)/shard_map/jk,ekc->ejc/dot_general | solution.py:45
  333.7 4.1 copy.100
  337.8 13.5 %all-to-all-start.5 = ((bf16[2,1,256,1088]{3,0,1,2:T(2,128)(2,1)}), bf16[2,1,256,1088]{3,0,1,2:T(2,128)(2,1)}, u32[]{:S(2)}, u32[]{:S(2)}) async-start(bf16[2,1,256,1088]{3,0,1,2:T(2,128)(2,1)} %copy.100), calls=%async_computation.7 | async-start | bytes 2359296 | tf_op jit(solution)/shard_map/all_to_all | solution.py:133
  351.3 4.2 fusion.21
  355.5 3.0 fusion.5
  358.5 2.8 copy.98
  361.2 21.2 %all-to-all-done.5 = bf16[2,1,256,1088]{3,0,1,2:T(2,128)(2,1)} async-done(((bf16[2,1,256,1088]{3,0,1,2:T(2,128)(2,1)}), bf16[2,1,256,1088]{3,0,1,2:T(2,128)(2,1)}, u32[]{:S(2)}, u32[]{:S(2)}) %all-to-all-start.5) | async-done | bytes 1114144 | tf_op jit(solution)/shard_map/all_to_all | solution.py:133
  382.4 6.5 %all-to-all-start.4 = ((bf16[2,1,256,1088]{3,0,1,2:T(2,128)(2,1)}), bf16[2,1,256,1088]{3,0,1,2:T(2,128)(2,1)S(1)}, u32[]{:S(2)}, u32[]{:S(2)}) async-start(bf16[2,1,256,1088]{3,0,1,2:T(2,128)(2,1)} %copy.98), calls=%async_computation.6 | async-start | bytes 2359296 | tf_op jit(solution)/shard_map/all_to_all | solution.py:130
  390.4 29.8 %all-to-all-done.4 = bf16[2,1,256,1088]{3,0,1,2:T(2,128)(2,1)S(1)} async-done(((bf16[2,1,256,1088]{3,0,1,2:T(2,128)(2,1)}), bf16[2,1,256,1088]{3,0,1,2:T(2,128)(2,1)S(1)}, u32[]{:S(2)}, u32[]{:S(2)}) %all-to-all-start.4) | async-done | bytes 1114144 | tf_op jit(solution)/shard_map/all_to_all | solution.py:130
  420.2 3.8 fusion.8
  424.0 2.6 fusion.10
  426.6 2.8 fusion.6
  429.4 1.9 copy.107
  431.3 6.6 %all-to-all-start.7 = ((bf16[2,64,4,1088]{3,2,0,1:T(4,128)(2,1)}), bf16[2,64,4,1088]{3,2,0,1:T(4,128)(2,1)S(1)}, u32[]{:S(2)}, u32[]{:S(2)}) async-start(bf16[2,64,4,1088]{3,2,0,1:T(4,128)(2,1)} %copy.107), calls=%async_computation.9 | async-start | bytes 2359296 | tf_op jit(solution)/shard_map/all_to_all | solution.py:142
  437.9 4.2 fusion.14
  442.1 2.8 fusion.7
  444.9 2.0 copy.104
  446.9 22.2 %all-to-all-done.7 = bf16[2,64,4,1088]{3,2,0,1:T(4,128)(2,1)S(1)} async-done(((bf16[2,64,4,1088]{3,2,0,1:T(4,128)(2,1)}), bf16[2,64,4,1088]{3,2,0,1:T(4,128)(2,1)S(1)}, u32[]{:S(2)}, u32[]{:S(2)}) %all-to-all-start.7) | async-done | bytes 1114144 | tf_op jit(solution)/shard_map/all_to_all | solution.py:142
  469.1 6.2 %all-to-all-start.6 = ((bf16[2,64,4,1088]{3,2,0,1:T(4,128)(2,1)}), bf16[2,64,4,1088]{3,2,0,1:T(4,128)(2,1)S(1)}, u32[]{:S(2)}, u32[]{:S(2)}) async-start(bf16[2,64,4,1088]{3,2,0,1:T(4,128)(2,1)} %copy.104), calls=%async_computation.8 | async-start | bytes 2359296 | tf_op jit(solution)/shard_map/all_to_all | solution.py:139
  475.4 1.8 fusion.258
  480.6 26.1 %all-to-all-done.6 = bf16[2,64,4,1088]{3,2,0,1:T(4,128)(2,1)S(1)} async-done(((bf16[2,64,4,1088]{3,2,0,1:T(4,128)(2,1)}), bf16[2,64,4,1088]{3,2,0,1:T(4,128)(2,1)S(1)}, u32[]{:S(2)}, u32[]{:S(2)}) %all-to-all-start.6) | async-done | bytes 1114144 | tf_op jit(solution)/shard_map/all_to_all | solution.py:139
  506.7 1.9 fusion.257
  510.3 2.6 squeeze.13
  516.8 3.0 fusion.28
  (114 shorter events, 50.7 us)
Async XLA Ops:
  7.2 2.4 copy-start.7
  7.2 2.4 copy-start.9
  19.5 1.0 copy-start.11
  22.9 41.7 %all-to-all-start = ((bf16[2,64,4,1024]{3,2,0,1:T(4,128)(2,1)}), bf16[2,64,4,1024]{3,2,0,1:T(4,128)(2,1)S(1)}, u32[]{:S(2)}, u32[]{:S(2)}) async-start(bf16[2,64,4,1024]{3,2,0,1:T(4,128)(2,1)} %copy.84), calls=%async_computation | async-start | bytes 2097152 | tf_op jit(solution)/shard_map/all_to_all | solution.py:95
  37.0 33.8 %copy-start.16 = (f32[256,16]{0,1:T(8,128)S(1)}, f32[256,16]{0,1:T(8,128)}, u32[]{:S(2)}) copy-start(f32[256,16]{0,1:T(8,128)} %param.12) | copy-start | bytes 49156
  37.0 33.9 %copy-start.17 = (f32[256,16]{0,1:T(8,128)S(1)}, f32[256,16]{0,1:T(8,128)}, u32[]{:S(2)}) copy-start(f32[256,16]{0,1:T(8,128)} %param.11) | copy-start | bytes 49156
  64.6 34.8 %all-to-all-start.1 = ((bf16[2,64,4,1024]{3,2,0,1:T(4,128)(2,1)}), bf16[2,64,4,1024]{3,2,0,1:T(4,128)(2,1)S(1)}, u32[]{:S(2)}, u32[]{:S(2)}) async-start(bf16[2,64,4,1024]{3,2,0,1:T(4,128)(2,1)} %copy.86), calls=%async_computation.1 | async-start | bytes 2097152 | tf_op jit(solution)/shard_map/all_to_all | solution.py:98
  74.2 39.2 %collective-permute-start = (bf16[2,256,256]{1,2,0:T(8,128)(2,1)S(1)}, bf16[2,256,256]{1,2,0:T(8,128)(2,1)}, u32[]{:S(2)}, u32[]{:S(2)}) collective-permute-start(bf16[2,256,256]{1,2,0:T(8,128)(2,1)S(1)} %fusion.55), channel_id=1, source_target_pairs={{0,4},{4,0},{8,12},{12,8},{16,20},{20,16},{24,28},{28,24},{32,36},... | collective-permute-start | bytes 786440 | tf_op jit(solution)/shard_map/ppermute | solution.py:26
  74.7 38.6 %collective-permute-start.1 = (bf16[2,256,256]{1,2,0:T(8,128)(2,1)S(1)}, bf16[2,256,256]{1,2,0:T(8,128)(2,1)}, u32[]{:S(2)}, u32[]{:S(2)}) collective-permute-start(bf16[2,256,256]{1,2,0:T(8,128)(2,1)S(1)} %pad_convert_fusion), channel_id=1, source_target_pairs={{0,4},{4,0},{8,12},{12,8},{16,20},{20,16},{24,28},{28,24},{32,36},... | collective-permute-start | bytes 786440 | tf_op jit(solution)/shard_map/ppermute | solution.py:26
  99.4 1.7 copy-start.2
  107.2 108.9 %all-to-all-start.2 = ((bf16[2,64,4,1024]{3,2,0,1:T(4,128)(2,1)}), bf16[2,64,4,1024]{3,2,0,1:T(4,128)(2,1)S(1)}, u32[]{:S(2)}, u32[]{:S(2)}) async-start(bf16[2,64,4,1024]{3,2,0,1:T(4,128)(2,1)} %copy.90), calls=%async_computation.2 | async-start | bytes 2097152 | tf_op jit(solution)/shard_map/all_to_all | solution.py:104
  115.6 27.8 %collective-permute-start.2 = (bf16[2,256,256]{1,2,0:T(8,128)(2,1)S(1)}, bf16[2,256,256]{1,2,0:T(8,128)(2,1)S(1)}, u32[]{:S(2)}, u32[]{:S(2)}) collective-permute-start(bf16[2,256,256]{1,2,0:T(8,128)(2,1)S(1)} %get-tuple-element.36), channel_id=1, source_target_pairs={{0,8},{8,0},{4,12},{12,4},{16,24},{24,16},{20,28},{28,20},{32,40},... | collective-permute-start | bytes 786440 | tf_op jit(solution)/shard_map/ppermute | solution.py:26
  117.0 32.0 %collective-permute-start.3 = (bf16[2,256,256]{1,2,0:T(8,128)(2,1)S(1)}, bf16[2,256,256]{1,2,0:T(8,128)(2,1)S(1)}, u32[]{:S(2)}, u32[]{:S(2)}) collective-permute-start(bf16[2,256,256]{1,2,0:T(8,128)(2,1)S(1)} %get-tuple-element.67), channel_id=1, source_target_pairs={{0,8},{8,0},{4,12},{12,4},{16,24},{24,16},{20,28},{28,20},{32,40},... | collective-permute-start | bytes 786440 | tf_op jit(solution)/shard_map/ppermute | solution.py:26
  143.4 5.6 %copy-start.13 = (bf16[2,256,256]{1,2,0:T(8,128)(2,1)}, bf16[2,256,256]{1,2,0:T(8,128)(2,1)S(1)}, u32[]{:S(2)}) copy-start(bf16[2,256,256]{1,2,0:T(8,128)(2,1)S(1)} %collective-permute-done.2) | copy-start | bytes 786436
  149.1 0.7 copy-start.15
  152.1 20.5 %collective-permute-start.4 = (bf16[2,256,256]{1,2,0:T(8,128)(2,1)}, bf16[2,256,256]{1,2,0:T(8,128)(2,1)}, u32[]{:S(2)}, u32[]{:S(2)}) collective-permute-start(bf16[2,256,256]{1,2,0:T(8,128)(2,1)} %get-tuple-element.32), channel_id=1, source_target_pairs={{0,16},{16,0},{4,20},{20,4},{8,24},{24,8},{12,28},{28,12},{32,48},... | collective-permute-start | bytes 786440 | tf_op jit(solution)/shard_map/ppermute | solution.py:26
  154.2 24.0 %collective-permute-start.5 = (bf16[2,256,256]{1,2,0:T(8,128)(2,1)S(1)}, bf16[2,256,256]{1,2,0:T(8,128)(2,1)}, u32[]{:S(2)}, u32[]{:S(2)}) collective-permute-start(bf16[2,256,256]{1,2,0:T(8,128)(2,1)S(1)} %get-tuple-element.65), channel_id=1, source_target_pairs={{0,16},{16,0},{4,20},{20,4},{8,24},{24,8},{12,28},{28,12},{32,48},... | collective-permute-start | bytes 786440 | tf_op jit(solution)/shard_map/ppermute | solution.py:26
  180.5 23.4 %collective-permute-start.6 = (bf16[2,256,256]{1,2,0:T(8,128)(2,1)}, bf16[2,256,256]{1,2,0:T(8,128)(2,1)S(1)}, u32[]{:S(2)}, u32[]{:S(2)}) collective-permute-start(bf16[2,256,256]{1,2,0:T(8,128)(2,1)} %get-tuple-element.28), channel_id=1, source_target_pairs={{0,32},{32,0},{4,36},{36,4},{8,40},{40,8},{12,44},{44,12},{16,48},... | collective-permute-start | bytes 786440 | tf_op jit(solution)/shard_map/ppermute | solution.py:26
  184.2 25.4 %collective-permute-start.7 = (bf16[2,256,256]{1,2,0:T(8,128)(2,1)S(1)}, bf16[2,256,256]{1,2,0:T(8,128)(2,1)S(1)}, u32[]{:S(2)}, u32[]{:S(2)}) collective-permute-start(bf16[2,256,256]{1,2,0:T(8,128)(2,1)S(1)} %get-tuple-element.63), channel_id=1, source_target_pairs={{0,32},{32,0},{4,36},{36,4},{8,40},{40,8},{12,44},{44,12},{16,48},... | collective-permute-start | bytes 786440 | tf_op jit(solution)/shard_map/ppermute | solution.py:26
  203.9 5.6 %copy-start.12 = (bf16[2,256,256]{1,2,0:T(8,128)(2,1)}, bf16[2,256,256]{1,2,0:T(8,128)(2,1)S(1)}, u32[]{:S(2)}) copy-start(bf16[2,256,256]{1,2,0:T(8,128)(2,1)S(1)} %collective-permute-done.6) | copy-start | bytes 786436
  209.6 0.7 copy-start.14
  212.6 11.8 %collective-permute-start.8 = (bf16[2,256,256]{1,2,0:T(8,128)(2,1)}, bf16[2,256,256]{1,2,0:T(8,128)(2,1)}, u32[]{:S(2)}, u32[]{:S(2)}) collective-permute-start(bf16[2,256,256]{1,2,0:T(8,128)(2,1)} %get-tuple-element.24), channel_id=1, source_target_pairs={{0,64},{64,0},{4,68},{68,4},{8,72},{72,8},{12,76},{76,12},{16,80},... | collective-permute-start | bytes 786440 | tf_op jit(solution)/shard_map/ppermute | solution.py:26
  214.0 11.6 %collective-permute-start.9 = (bf16[2,256,256]{1,2,0:T(8,128)(2,1)S(1)}, bf16[2,256,256]{1,2,0:T(8,128)(2,1)}, u32[]{:S(2)}, u32[]{:S(2)}) collective-permute-start(bf16[2,256,256]{1,2,0:T(8,128)(2,1)S(1)} %get-tuple-element.61), channel_id=1, source_target_pairs={{0,64},{64,0},{4,68},{68,4},{8,72},{72,8},{12,76},{76,12},{16,80},... | collective-permute-start | bytes 786440 | tf_op jit(solution)/shard_map/ppermute | solution.py:26
  216.0 51.0 %all-to-all-start.3 = ((bf16[2,64,4,1024]{3,2,0,1:T(4,128)(2,1)}), bf16[2,64,4,1024]{3,2,0,1:T(4,128)(2,1)S(1)}, u32[]{:S(2)}, u32[]{:S(2)}) async-start(bf16[2,64,4,1024]{3,2,0,1:T(4,128)(2,1)} %copy.93), calls=%async_computation.3 | async-start | bytes 2097152 | tf_op jit(solution)/shard_map/all_to_all | solution.py:107
  224.4 76.5 %reduce-scatter.5.cloned.1.call-start = ((), (), s32[]{:S(2)}) async-start(), calls=%async_computation.11 | async-start | bytes 327680 | tf_op jit(solution)/shard_map/reduce_scatter | solution.py:223
  227.9 13.5 %collective-permute-start.10 = (bf16[2,256,256]{1,2,0:T(8,128)(2,1)}, bf16[2,256,256]{1,2,0:T(8,128)(2,1)S(1)}, u32[]{:S(2)}, u32[]{:S(2)}) collective-permute-start(bf16[2,256,256]{1,2,0:T(8,128)(2,1)} %get-tuple-element.20), channel_id=1, source_target_pairs={{0,128},{128,0},{4,132},{132,4},{8,136},{136,8},{12,140},{140,12},... | collective-permute-start | bytes 786440 | tf_op jit(solution)/shard_map/ppermute | solution.py:26
  230.8 21.1 %collective-permute-start.11 = (bf16[2,256,256]{1,2,0:T(8,128)(2,1)S(1)}, bf16[2,256,256]{1,2,0:T(8,128)(2,1)S(1)}, u32[]{:S(2)}, u32[]{:S(2)}) collective-permute-start(bf16[2,256,256]{1,2,0:T(8,128)(2,1)S(1)} %get-tuple-element.59), channel_id=1, source_target_pairs={{0,128},{128,0},{4,132},{132,4},{8,136},{136,8},{12,140},{140,12},... | collective-permute-start | bytes 786440 | tf_op jit(solution)/shard_map/ppermute | solution.py:26
  269.2 2.0 copy-start.1
  273.2 2.1 copy-start.3
  273.2 2.1 copy-start.4
  279.8 47.2 %reduce-scatter.3.cloned.1.call-start = ((), (), s32[]{:S(2)}) async-start(), calls=%async_computation.10 | async-start | bytes 327680 | tf_op jit(solution)/shard_map/reduce_scatter | solution.py:220
  337.8 44.6 %all-to-all-start.5 = ((bf16[2,1,256,1088]{3,0,1,2:T(2,128)(2,1)}), bf16[2,1,256,1088]{3,0,1,2:T(2,128)(2,1)}, u32[]{:S(2)}, u32[]{:S(2)}) async-start(bf16[2,1,256,1088]{3,0,1,2:T(2,128)(2,1)} %copy.100), calls=%async_computation.7 | async-start | bytes 2359296 | tf_op jit(solution)/shard_map/all_to_all | solution.py:133
  382.4 37.8 %all-to-all-start.4 = ((bf16[2,1,256,1088]{3,0,1,2:T(2,128)(2,1)}), bf16[2,1,256,1088]{3,0,1,2:T(2,128)(2,1)S(1)}, u32[]{:S(2)}, u32[]{:S(2)}) async-start(bf16[2,1,256,1088]{3,0,1,2:T(2,128)(2,1)} %copy.98), calls=%async_computation.6 | async-start | bytes 2359296 | tf_op jit(solution)/shard_map/all_to_all | solution.py:130
  424.0 2.6 copy-start
  431.3 37.8 %all-to-all-start.7 = ((bf16[2,64,4,1088]{3,2,0,1:T(4,128)(2,1)}), bf16[2,64,4,1088]{3,2,0,1:T(4,128)(2,1)S(1)}, u32[]{:S(2)}, u32[]{:S(2)}) async-start(bf16[2,64,4,1088]{3,2,0,1:T(4,128)(2,1)} %copy.107), calls=%async_computation.9 | async-start | bytes 2359296 | tf_op jit(solution)/shard_map/all_to_all | solution.py:142
  469.1 37.6 %all-to-all-start.6 = ((bf16[2,64,4,1088]{3,2,0,1:T(4,128)(2,1)}), bf16[2,64,4,1088]{3,2,0,1:T(4,128)(2,1)S(1)}, u32[]{:S(2)}, u32[]{:S(2)}) async-start(bf16[2,64,4,1088]{3,2,0,1:T(4,128)(2,1)} %copy.104), calls=%async_computation.8 | async-start | bytes 2359296 | tf_op jit(solution)/shard_map/all_to_all | solution.py:139
  514.7 2.1 copy-start.5
  514.7 2.1 copy-start.6
  514.7 2.1 copy-start.8
  514.7 2.1 copy-start.10
  514.8 2.1 copy-start.18
Sparse Core Ops, SparseCore 0:
  279.9 20.8 reduce-scatter.4
  304.1 22.8 reduce-scatter.2
where the time goes:
time: 536 us; the launch traced here: 527 us
  waiting for transfers between devices  286 us (53%)
  starting transfers between devices  82.3 us (15%)
  matrix products  55.9 us (10%)
  local copies, waits for them, and re-layouts  47.8 us (9%)
  other arithmetic  39 us (7%)
  between operations  16 us (3%)
    ppermute x12, waiting for transfers between devices, partner(): return lax.ppermute(block, axis, route)  100 us
    all_to_all x1, waiting for transfers between devices, spread_inverse(): lax.all_to_all(for_sending(rows_re), 'seq', split_axis=2, concat_axis=1,...  29.8 us
    all_to_all x1, waiting for transfers between devices, spread_inverse(): lax.all_to_all(for_sending(cross_re), 'seq', split_axis=1, concat_axis=2,...  26.1 us
    all_to_all x1, waiting for transfers between devices, spread_forward(): lax.all_to_all(signal_re.astype(jnp.bfloat16), 'seq', split_axis=1, conca...  26 us
    all_to_all x1, waiting for transfers between devices, spread_inverse(): lax.all_to_all(for_sending(cross_im), 'seq', split_axis=1, concat_axis=2,...  22.2 us
    all_to_all x1, waiting for transfers between devices, spread_inverse(): lax.all_to_all(for_sending(rows_im), 'seq', split_axis=2, concat_axis=1,...  21.2 us
    reduce_scatter x1, waiting for transfers between devices, sequence_layout(): lax.psum_scatter(cross_re.astype(jnp.bfloat16), 'chan', scatter_dimension...  21.1 us
    all_to_all x1, waiting for transfers between devices, spread_forward(): lax.all_to_all(signal_im.astype(jnp.bfloat16), 'seq', split_axis=1, conca...  20.8 us
  transfers between devices with their start and end apart: 22, of which 17 were waited for; matrix products, arithmetic and copies ran while one was open for 15% of the time, Pallas kernels for 0%

commit v1 on v0

v1 whole, which is shorter than its diff:
```python
import math

import jax
import jax.numpy as jnp
from jax import lax
from jax.experimental import pallas as pl
from jax.experimental.pallas import tpu as pltpu
from jax.sharding import PartitionSpec as P

CHANNELS = 4096
FILTERS = 256
MODES = 16
SEQ_LEN = 16384
SHARDS = 64
ROWS = 256
GROUPS = 4
F32 = jnp.float32
BF16 = jnp.bfloat16
LANES = 128
STEPS = 32
SUBS = 8
TILES = 8
ACROSS = (((1,), (1,)), ((), ()))


def iota(shape, dim):
    return lax.broadcasted_iota(jnp.int32, shape, dim)


def identity(size):
    return (iota((size, size), 0) == iota((size, size), 1)).astype(BF16)


def reversal(size):
    row, col = iota((size, size), 0), iota((size, size), 1)
    return ((row + col == size) | ((row == 0) & (col == 0))).astype(BF16)


def load_signals(q_ref, k_ref, v_ref, o_ref, sig_ref):
    for tile in range(TILES):
        lanes = pl.ds(tile * LANES, LANES)
        conv_in = (k_ref[:, lanes].astype(F32) * v_ref[:, lanes].astype(F32)).astype(BF16)
        mid_grad = (o_ref[:, lanes].astype(F32) * q_ref[:, lanes].astype(F32)).astype(BF16)
        sig_ref[0, tile] = conv_in.astype(F32)
        sig_ref[1, tile] = mid_grad.astype(F32)


def pack_chunk(chunk, sig_ref, spread_ref, pack_ref):
    eye = identity(LANES)
    rev = reversal(LANES)
    for group in range(GROUPS):
        tile = 2 * group + chunk
        for sig in range(2):
            for half in range(2):
                block = sig_ref[sig, tile, half * LANES:(half + 1) * LANES, :].astype(BF16)
                if sig == 0:
                    block = jnp.dot(rev, block, preferred_element_type=F32).astype(BF16)
                turned = lax.dot_general(eye, block, ACROSS, preferred_element_type=F32)
                for low in range(2):
                    place = sig * 8 + low * 4 + group
                    spread_ref[half, pl.ds(place, SHARDS, stride=16), :] = turned[
                        low * SHARDS:(low + 1) * SHARDS
                    ]
    for half in range(2):
        pack_ref[chunk, :, half * LANES:(half + 1) * LANES] = spread_ref[half].astype(BF16)


def make_decays(rates_ref, weights_ref, base_ref, gain_ref):
    for side in range(2):
        for mode in range(MODES):
            rate = jnp.broadcast_to(rates_ref[side, mode:mode + 1, :], (SUBS, LANES))
            base_ref[side, mode] = jnp.exp(-rate)
            gain_ref[side, mode] = jnp.broadcast_to(
                weights_ref[side, mode:mode + 1, :], (SUBS, LANES)
            ) * jnp.sqrt(rate)


def block_states(sig_ref, rates_ref, base_ref, ends_ref, state_ref):
    sub = iota((SUBS, LANES), 0).astype(F32)

    def one_group(group, _):
        for side in range(2):
            tile = 2 * group + side
            base = [base_ref[side, mode] for mode in range(MODES)]
            for sig in range(2):
                acc = None
                for step in range(STEPS):
                    place = step if sig == 0 else STEPS - 1 - step
                    row = sig_ref[sig, tile, pl.ds(place, SUBS, stride=STEPS), :]
                    if acc is None:
                        acc = [row] * MODES
                    else:
                        acc = [b * a + row for b, a in zip(base, acc)]
                steps_left = (SUBS - 1.0 - sub if sig == 0 else sub) * float(STEPS)
                for mode in range(MODES):
                    ends_ref[sig, tile, mode] = acc[mode]
                    rate = rates_ref[side, mode:mode + 1, :]
                    whole = jnp.sum(acc[mode] * jnp.exp(-rate * steps_left), axis=0, keepdims=True)
                    state_ref[mode * GROUPS + group, sig * 2 + side:sig * 2 + side + 1, :] = whole
        return _
    lax.fori_loop(0, GROUPS, one_group, 0)


def scan_blocks(mode, rates_ref, got_ref, enter_ref):
    decay = [
        jnp.exp(-float(ROWS) * rates_ref[side, pl.ds(mode, 1), :]) for side in range(2)
    ]

    def step(at, held):
        back = SHARDS - 1 - at
        out = []
        for sig in range(2):
            place = at if sig == 0 else back
            for side in range(2):
                now = held[sig * 2 + side]
                rows = slice(sig * 2 + side, sig * 2 + side + 1)
                enter_ref[place, rows, :] = now
                out.append(decay[side] * now + got_ref[place, rows, :])
        return tuple(out)
    lax.fori_loop(0, SHARDS, step, (jnp.zeros((1, LANES), F32),) * 4)


def run_recurrence(sig_ref, rates_ref, base_ref, gain_ref, ends_ref, enter_ref, long_ref):
    sub = iota((SUBS, LANES), 0)

    def one_group(group, _):
        for side in range(2):
            tile = 2 * group + side
            base = [base_ref[side, mode] for mode in range(MODES)]
            gain = [gain_ref[side, mode] for mode in range(MODES)]
            for sig in range(2):
                held = []
                for mode in range(MODES):
                    rate = rates_ref[side, mode:mode + 1, :]
                    first = enter_ref[mode * GROUPS + group, sig * 2 + side:sig * 2 + side + 1, :]
                    ends = ends_ref[sig, tile, mode]
                    if sig == 0:
                        state = jnp.where(sub == 0, first, pltpu.roll(ends, 1, 0))
                    else:
                        state = jnp.where(sub == SUBS - 1, first, pltpu.roll(ends, SUBS - 1, 0))
                    for hop in (1, 2, 4):
                        decay = jnp.exp(-float(STEPS * hop) * rate)
                        if sig == 0:
                            moved = jnp.where(sub >= hop, pltpu.roll(state, hop, 0), 0.0)
                        else:
                            moved = jnp.where(sub < SUBS - hop, pltpu.roll(state, SUBS - hop, 0), 0.0)
                        state = state + decay * moved
                    held.append(state)
                for step in range(STEPS):
                    place = step if sig == 0 else STEPS - 1 - step
                    where = pl.ds(place, SUBS, stride=STEPS)
                    row = sig_ref[sig, tile, where, :]
                    held = [b * h + row for b, h in zip(base, held)]
                    terms = [w * h for w, h in zip(gain, held)]
                    while len(terms) > 1:
                        terms = [a + b for a, b in zip(terms[::2], terms[1::2])]
                    long_ref[sig, tile, where, :] = terms[0]
        return _
    lax.fori_loop(0, GROUPS, one_group, 0)


def finish_outputs(q_ref, k_ref, v_ref, skip_ref, sig_ref, long_ref, layer_ref, kgrad_ref, vgrad_ref):
    for tile in range(TILES):
        lanes = pl.ds(tile * LANES, LANES)
        skip = skip_ref[:, lanes]
        layer = long_ref[0, tile] + skip * sig_ref[0, tile]
        layer_ref[:, lanes] = (q_ref[:, lanes].astype(F32) * layer).astype(BF16)
        total = long_ref[1, tile] + skip * sig_ref[1, tile]
        kgrad_ref[:, lanes] = (total * v_ref[:, lanes].astype(F32)).astype(BF16)
        vgrad_ref[:, lanes] = (total * k_ref[:, lanes].astype(F32)).astype(BF16)


PAD = ROWS
WINDOW = 528


def correlate_filter(chunk, low, got_ref, rows_ref, slide_ref, slid_ref, grad_ref, turn_ref, keep_ref, sums_ref, out_ref):
    eye = identity(ROWS)
    for half in range(2):
        lanes = slice(half * LANES, (half + 1) * LANES)
        for group in range(GROUPS):
            conv_rows = rows_ref[half, pl.ds(low * 4 + group, SHARDS, stride=16), :]
            for early in range(4):
                slide_ref[early, half, pl.ds(PAD + group + 4 * early, SHARDS, stride=4), :] = conv_rows
            grad_ref[half, pl.ds(group, SHARDS, stride=4), :] = rows_ref[
                half, pl.ds(8 + low * 4 + group, SHARDS, stride=16), :
            ]
        for early in range(4):
            slid_ref[early, :, lanes] = slide_ref[early, half, :2 * ROWS, :].astype(BF16)
        turn_ref[lanes, :] = lax.dot_general(
            identity(LANES), grad_ref[half].astype(BF16), ACROSS, preferred_element_type=F32
        ).astype(BF16)

    row, lane = iota((LANES, LANES), 0), iota((LANES, LANES), 1)
    causal = (lane == 0) | (row + lane >= LANES)
    turn = turn_ref[...]
    keep_ref[...] = jnp.zeros_like(keep_ref)

    def sheared(block):
        total = block[:SUBS]
        for part in range(1, LANES // SUBS):
            total = total + pltpu.roll(block[part * SUBS:(part + 1) * SUBS], part * SUBS, 1)
        return total

    def four_lags(at, _):
        far = SHARDS // 4 - 1 - at
        for early in (3, 2, 1, 0):
            start = pl.multiple_of(PAD - 16 * far, 16)
            window = slid_ref[early, pl.ds(start, ROWS), :]
            prod = jnp.dot(turn, window, preferred_element_type=F32)
            odd = prod[LANES:, :LANES] + keep_ref[0]
            even = prod[:LANES, :LANES] + prod[LANES:, LANES:]
            odd_row = jnp.where(causal, odd, keep_ref[1])
            even_row = jnp.where(causal, even, odd)
            keep_ref[0] = prod[:LANES, LANES:]
            keep_ref[1] = even
            sums_ref[4 * far + early, 0] = sheared(even_row)
            sums_ref[4 * far + early, 1] = sheared(odd_row)
        return _
    lax.fori_loop(0, SHARDS // 4, four_lags, 0)

    def gather(at, _):
        for part in range(2):
            block = pltpu.roll(sums_ref[at, part], 0, 1, stride=1, stride_axis=0)
            out_ref[2 * chunk + low, at, part:part + 1, :] = jnp.sum(block, axis=0, keepdims=True)
        return _
    lax.fori_loop(0, SHARDS, gather, 0)


def prep_kernel(q_ref, k_ref, v_ref, o_ref, rates_ref, weights_ref, pack_ref, state_ref, ends_ref,
                sig_ref, spread_ref, base_ref, gain_ref):
    load_signals(q_ref, k_ref, v_ref, o_ref, sig_ref)
    for chunk in range(2):
        pack_chunk(chunk, sig_ref, spread_ref, pack_ref)
    make_decays(rates_ref, weights_ref, base_ref, gain_ref)
    block_states(sig_ref, rates_ref, base_ref, ends_ref, state_ref)


def scan_kernel(rates_ref, got_ref, enter_ref):
    mode = lax.axis_index("seq") // GROUPS
    scan_blocks(mode, rates_ref, got_ref, enter_ref)


def output_kernel(q_ref, k_ref, v_ref, o_ref, rates_ref, weights_ref, skip_ref, ends_ref, enter_ref,
                  layer_ref, kgrad_ref, vgrad_ref, sig_ref, base_ref, gain_ref, long_ref):
    load_signals(q_ref, k_ref, v_ref, o_ref, sig_ref)
    make_decays(rates_ref, weights_ref, base_ref, gain_ref)
    run_recurrence(sig_ref, rates_ref, base_ref, gain_ref, ends_ref, enter_ref, long_ref)
    finish_outputs(q_ref, k_ref, v_ref, skip_ref, sig_ref, long_ref, layer_ref, kgrad_ref, vgrad_ref)


def correlate_kernel(got_ref, out_ref, rows_ref, slide_ref, slid_ref, grad_ref, turn_ref, keep_ref, sums_ref):
    slide_ref[...] = jnp.zeros_like(slide_ref)
    for chunk in range(2):
        for half in range(2):
            rows_ref[half] = got_ref[chunk, :, half * LANES:(half + 1) * LANES].astype(F32)
        for low in range(2):
            correlate_filter(
                chunk, low, got_ref, rows_ref, slide_ref, slid_ref, grad_ref, turn_ref, keep_ref, sums_ref, out_ref
            )


CORRELATE_SCRATCH = [
    pltpu.VMEM((2, SHARDS * 16, LANES), F32),
    pltpu.VMEM((4, 2, WINDOW, LANES), F32),
    pltpu.VMEM((4, 2 * ROWS, ROWS), BF16),
    pltpu.VMEM((2, ROWS, LANES), F32),
    pltpu.VMEM((ROWS, ROWS), BF16),
    pltpu.VMEM((2, LANES, LANES), F32),
    pltpu.VMEM((SHARDS, 2, SUBS, LANES), F32),
]
SIGNALS = pltpu.VMEM((2, TILES, ROWS, LANES), F32)
DECAYS = pltpu.VMEM((2, MODES, SUBS, LANES), F32)
VMEM = pl.BlockSpec(memory_space=pltpu.VMEM)


def call(kernel, shapes, scratch, count):
    return pl.pallas_call(
        kernel,
        out_shape=shapes,
        in_specs=[VMEM] * count,
        out_specs=jax.tree.map(lambda _: VMEM, shapes),
        scratch_shapes=scratch,
        compiler_params=pltpu.CompilerParams(vmem_limit_bytes=56 * 2**20),
    )


def per_device(query_proj, key_proj, value_proj, out_grad, residues, decay_rate, skip_gain):
    sds = jax.ShapeDtypeStruct
    rates = decay_rate.reshape(2, LANES, MODES).transpose(0, 2, 1)
    weights = residues.reshape(2, LANES, MODES).transpose(0, 2, 1)
    pack, state, ends = call(
        prep_kernel,
        (sds((2, SHARDS * 16, ROWS), BF16), sds((SHARDS, 4, LANES), F32), sds((2, TILES, MODES, SUBS, LANES), F32)),
        [SIGNALS, pltpu.VMEM((2, SHARDS * 16, LANES), F32), DECAYS, DECAYS],
        6,
    )(query_proj, key_proj, value_proj, out_grad, rates, weights)
    got = lax.all_to_all(state, "seq", split_axis=0, concat_axis=0, tiled=True)
    arrived = lax.all_to_all(
        pack.reshape(2, SHARDS, 16, ROWS), "seq", split_axis=1, concat_axis=1, tiled=True
    ).reshape(2, SHARDS * 16, ROWS)
    enter = call(scan_kernel, sds((SHARDS, 4, LANES), F32), [], 2)(rates, got)
    enter = lax.all_to_all(enter, "seq", split_axis=0, concat_axis=0, tiled=True)
    layer, kgrad, vgrad = call(
        output_kernel,
        (sds((ROWS, 1024), BF16),) * 3,
        [SIGNALS, DECAYS, DECAYS, SIGNALS],
        9,
    )(query_proj, key_proj, value_proj, out_grad, rates, weights, skip_gain[None, :], ends, enter)
    shares = call(correlate_kernel, sds((4, SHARDS, 2, LANES), F32), CORRELATE_SCRATCH, 1)(arrived)
    shares = lax.all_to_all(shares, "chan", split_axis=0, concat_axis=0, tiled=True)
    taps = shares.sum(axis=0)
    taps = lax.all_to_all(taps, "seq", split_axis=0, concat_axis=0, tiled=True)
    scale = 1.0 / math.sqrt(SEQ_LEN * (CHANNELS // FILTERS))
    filter_grad = taps.reshape(SHARDS, ROWS).T * scale
    return (layer, kgrad, vgrad, filter_grad)


def solution(mesh):
    wide = P("seq", "chan")
    return jax.shard_map(
        per_device,
        mesh=mesh,
        in_specs=(wide, wide, wide, wide, P(), P(), P("chan")),
        out_specs=(wide, wide, wide, wide),
        check_vma=False,
    )
```

time: 536 us -> 161 us (0.30); the launches traced: 527 us -> 160 us
  waiting for transfers between devices: 286 us -> 13.2 us
  Pallas kernels: 0 us -> 71 us
  matrix products: 55.9 us -> 0 us
  starting transfers between devices: 82.3 us -> 27 us
  local copies, waits for them, and re-layouts: 47.8 us -> 5.77 us
  blocking collectives: 0 us -> 41.5 us
  other arithmetic: 39 us -> 0.77 us
  between operations: 16 us -> 0.69 us
    all_to_all x8 -> x4, waiting for transfers between devices: 146 us -> 13.2 us  [the longest x1 9.63 us: per_device(): lax.all_to_all(enter, 'seq', split_axis=0, concat_axis=0, tiled=True)]
    ppermute x12 -> x0, waiting for transfers between devices: 100 us -> none  [partner(): return lax.ppermute(block, axis, route)]
    pallas_call x0 -> x4, Pallas kernels: none -> 71 us  [the longest x1 50.5 us: per_device(): call(correlate_kernel, sds((4, SHARDS, 2, LANES), F32), CORRELATE_SCRATCH...]
    dot_general x20 -> x0, matrix products: 55.9 us -> none  [the longest x5 16.4 us: complex_mix(): jnp.einsum(pattern, matrix_re, values_re, precision=PRECISE)]
    all_to_all x0 -> x1, blocking collectives: none -> 41.5 us  [per_device(): lax.all_to_all(pack.reshape(2, SHARDS, 16, ROWS), 'seq', split_axis=1, co...]
    all_to_all x8 -> x4, starting transfers between devices: 66.6 us -> 27 us  [the longest x1 11.9 us: per_device(): lax.all_to_all(enter, 'seq', split_axis=0, concat_axis=0, tiled=True)]
    reduce_scatter x2 -> x0, waiting for transfers between devices: 39.5 us -> none  [the longest x1 21.1 us: sequence_layout(): lax.psum_scatter(cross_re.astype(jnp.bfloat16), 'chan', scatter_dimension...]
    convert_element_type x12 -> x0, other arithmetic: 17.9 us -> none  [the longest x6 11.6 us: butterfly_spectrum(): state_re.astype(jnp.bfloat16)]
  transfers between devices with their start and end apart: 22 -> 4, of which waited for: 17 -> 2; matrix products, arithmetic and copies ran while one was open for 15% -> 1% of each run, Pallas kernels for 0% -> 39%
where the time goes in v1:
time: 161 us; the launch traced here: 160 us
  Pallas kernels  71 us (44%)
  blocking collectives  41.5 us (26%)
  starting transfers between devices  27 us (17%)
  waiting for transfers between devices  13.2 us (8%)
  local copies, waits for them, and re-layouts  5.77 us (4%)
    pallas_call x1, Pallas kernels, per_device(): call(correlate_kernel, sds((4, SHARDS, 2, LANES), F32), CORRELATE_SCRATCH...  50.5 us
    all_to_all x1, blocking collectives, per_device(): lax.all_to_all(pack.reshape(2, SHARDS, 16, ROWS), 'seq', split_axis=1, co...  41.5 us
    all_to_all x1, starting transfers between devices, per_device(): lax.all_to_all(enter, 'seq', split_axis=0, concat_axis=0, tiled=True)  11.9 us
    pallas_call x1, Pallas kernels, per_device(): call(output_kernel, (sds((ROWS, 1024), BF16),) * 3, [SIGNALS, DECAYS, DEC...  9.86 us
    all_to_all x1, waiting for transfers between devices, per_device(): lax.all_to_all(enter, 'seq', split_axis=0, concat_axis=0, tiled=True)  9.63 us
    pallas_call x1, Pallas kernels, per_device(): call(prep_kernel, (sds((2, SHARDS * 16, ROWS), BF16), sds((SHARDS, 4, LAN...  8.56 us
    all_to_all x1, starting transfers between devices, per_device(): got = lax.all_to_all(state, 'seq', split_axis=0, concat_axis=0, tiled=True)  6.19 us
    all_to_all x1, starting transfers between devices, per_device(): taps = lax.all_to_all(taps, 'seq', split_axis=0, concat_axis=0, tiled=True)  4.89 us
  transfers between devices with their start and end apart: 4, of which 2 were waited for; matrix products, arithmetic and copies ran while one was open for 1% of the time, Pallas kernels for 39%

profile of v1, /device:TPU:1, one launch (start us, length us, event | category | flops | bytes accessed | tf_op | source)
XLA Modules:
  0.0 160.0 jit_solution(17080615377968020249)
XLA Ops:
  0.6 0.0 copy-start
  0.6 0.7 copy-done
  1.4 1.3 bitcast_bitcast_fusion.1
  2.7 8.6 %shard_map.102 = (bf16[2,1024,256]{2,1,0:T(8,128)(2,1)}, f32[64,4,128]{2,1,0:T(4,128)}, f32[2,8,16,8,128]{4,3,2,1,0:T(8,128)}) custom-call(bf16[256,1024]{1,0:T(8,128)(2,1)} %q_ref.3, bf16[256,1024]{1,0:T(8,128)(2,1)} %k_ref.3, bf16[256,1024]{1,0:T(8,128)(2,1)} %v_ref.3, bf16[256,1024]{1,0:T(8,128)(2,1)} %o_ref.3, ...), custom_call_target="tpu_custom_call" | custom-call | tf_op jit(solution)/shard_map/pallas_call | solution.py:292
  11.2 1.4 copy.15
  12.6 41.5 %all_to_all.25 = bf16[2,64,16,256]{3,2,0,1:T(8,128)(2,1)S(1)} all-to-all(bf16[2,64,16,256]{3,2,0,1:T(8,128)(2,1)S(1)} %copy.15), channel_id=1, replica_groups=mesh['seq'=64,'chan'=4] {'seq'}, dimensions={1} | all-to-all | bytes 2097152 | tf_op jit(solution)/shard_map/all_to_all | solution.py:299
  54.1 6.2 %all-to-all-start = ((f32[64,4,128]{2,1,0:T(4,128)}), f32[64,4,128]{2,1,0:T(4,128)S(1)}, u32[]{:S(2)}, u32[]{:S(2)}) async-start(f32[64,4,128]{2,1,0:T(4,128)} %get-tuple-element.11), calls=%async_computation | async-start | bytes 262144 | tf_op jit(solution)/shard_map/all_to_all | solution.py:298
  60.3 1.1 copy.16
  61.4 50.5 %shard_map.105 = f32[4,64,2,128]{3,2,1,0:T(2,128)} custom-call(bf16[2,1024,256]{2,1,0:T(8,128)(2,1)} %bitcast.24), custom_call_target="tpu_custom_call" | custom-call | tf_op jit(solution)/shard_map/pallas_call | solution.py:310
  111.9 0.0 all-to-all-done.got_ref
  111.9 0.0 copy-start.2
  111.9 0.7 copy-done.2
  112.6 4.0 %all-to-all-start.3 = ((f32[4,64,2,128]{3,2,1,0:T(2,128)}), f32[4,64,2,128]{3,2,1,0:T(2,128)S(1)}, u32[]{:S(2)}, u32[]{:S(2)}) async-start(f32[4,64,2,128]{3,2,1,0:T(2,128)} %shard_map.105), calls=%async_computation.3 | async-start | bytes 524288 | tf_op jit(solution)/shard_map/all_to_all | solution.py:311
  116.6 2.1 %shard_map.103 = f32[64,4,128]{2,1,0:T(4,128)} custom-call(f32[2,16,128]{2,1,0:T(8,128)} %get-tuple-element.17.rates_ref, f32[64,4,128]{2,1,0:T(4,128)} %copy-done.2), custom_call_target="tpu_custom_call" | custom-call | tf_op jit(solution)/shard_map/pallas_call | solution.py:302
  118.7 3.6 %all-to-all-done.3 = f32[4,64,2,128]{3,2,1,0:T(2,128)S(1)} async-done(((f32[4,64,2,128]{3,2,1,0:T(2,128)}), f32[4,64,2,128]{3,2,1,0:T(2,128)S(1)}, u32[]{:S(2)}, u32[]{:S(2)}) %all-to-all-start.3) | async-done | bytes 262176 | tf_op jit(solution)/shard_map/all_to_all | solution.py:311
  122.3 11.9 %all-to-all-start.1 = ((f32[64,4,128]{2,1,0:T(4,128)}), f32[64,4,128]{2,1,0:T(4,128)S(1)}, u32[]{:S(2)}, u32[]{:S(2)}) async-start(f32[64,4,128]{2,1,0:T(4,128)} %shard_map.103), calls=%async_computation.1 | async-start | bytes 262144 | tf_op jit(solution)/shard_map/all_to_all | solution.py:303
  134.2 0.7 reduce_sum.9
  134.9 9.6 %all-to-all-done.1.enter_ref = f32[64,4,128]{2,1,0:T(4,128)S(1)} async-done(((f32[64,4,128]{2,1,0:T(4,128)}), f32[64,4,128]{2,1,0:T(4,128)S(1)}, u32[]{:S(2)}, u32[]{:S(2)}) %all-to-all-start.1) | async-done | bytes 131104 | tf_op jit(solution)/shard_map/all_to_all | solution.py:303
  144.5 0.0 copy-start.1
  144.5 4.9 %all-to-all-start.4 = ((f32[64,2,128]{2,1,0:T(2,128)}), f32[64,2,128]{2,1,0:T(2,128)S(1)}, u32[]{:S(2)}, u32[]{:S(2)}) async-start(f32[64,2,128]{2,1,0:T(2,128)} %reduce_sum.9), calls=%async_computation.4 | async-start | bytes 131072 | tf_op jit(solution)/shard_map/all_to_all | solution.py:313
  149.4 0.0 copy-done.1
  149.4 9.9 %shard_map.104 = (bf16[256,1024]{1,0:T(8,128)(2,1)}, bf16[256,1024]{1,0:T(8,128)(2,1)}, bf16[256,1024]{1,0:T(8,128)(2,1)}) custom-call(bf16[256,1024]{1,0:T(8,128)(2,1)} %q_ref.3, bf16[256,1024]{1,0:T(8,128)(2,1)} %k_ref.3, bf16[256,1024]{1,0:T(8,128)(2,1)} %v_ref.3, bf16[256,1024]{1,0:T(8,128)(2,1)} %o_ref.3, f32[2,16,128]{2,1,0:T(8,128)} %get-tuple-element.17.rates_ref, ...), custom_call_target="tpu_custom_call" | custom-call | tf_op jit(solution)/shard_map/pallas_call | solution.py:304
  159.3 0.0 all-to-all-done.4
  159.3 0.6 copy.23
  (1 shorter events, 0.0 us)
Async XLA Ops:
  0.6 0.7 copy-start
  54.1 57.8 %all-to-all-start = ((f32[64,4,128]{2,1,0:T(4,128)}), f32[64,4,128]{2,1,0:T(4,128)S(1)}, u32[]{:S(2)}, u32[]{:S(2)}) async-start(f32[64,4,128]{2,1,0:T(4,128)} %get-tuple-element.11), calls=%async_computation | async-start | bytes 262144 | tf_op jit(solution)/shard_map/all_to_all | solution.py:298
  111.9 0.7 copy-start.2
  112.6 9.7 %all-to-all-start.3 = ((f32[4,64,2,128]{3,2,1,0:T(2,128)}), f32[4,64,2,128]{3,2,1,0:T(2,128)S(1)}, u32[]{:S(2)}, u32[]{:S(2)}) async-start(f32[4,64,2,128]{3,2,1,0:T(2,128)} %shard_map.105), calls=%async_computation.3 | async-start | bytes 524288 | tf_op jit(solution)/shard_map/all_to_all | solution.py:311
  122.3 22.2 %all-to-all-start.1 = ((f32[64,4,128]{2,1,0:T(4,128)}), f32[64,4,128]{2,1,0:T(4,128)S(1)}, u32[]{:S(2)}, u32[]{:S(2)}) async-start(f32[64,4,128]{2,1,0:T(4,128)} %shard_map.103), calls=%async_computation.1 | async-start | bytes 262144 | tf_op jit(solution)/shard_map/all_to_all | solution.py:303
  144.5 4.9 %copy-start.1 = (f32[64,4,128]{2,1,0:T(4,128)}, f32[64,4,128]{2,1,0:T(4,128)S(1)}, u32[]{:S(2)}) copy-start(f32[64,4,128]{2,1,0:T(4,128)S(1)} %all-to-all-done.1.enter_ref) | copy-start | bytes 393220
  144.5 14.8 %all-to-all-start.4 = ((f32[64,2,128]{2,1,0:T(2,128)}), f32[64,2,128]{2,1,0:T(2,128)S(1)}, u32[]{:S(2)}, u32[]{:S(2)}) async-start(f32[64,2,128]{2,1,0:T(2,128)} %reduce_sum.9), calls=%async_computation.4 | async-start | bytes 131072 | tf_op jit(solution)/shard_map/all_to_all | solution.py:313

commit v2 on v1

v2 whole, which is shorter than its diff:
```python
import math

import jax
import jax.numpy as jnp
from jax import lax
from jax.experimental import pallas as pl
from jax.experimental.pallas import tpu as pltpu
from jax.sharding import PartitionSpec as P

CHANNELS = 4096
FILTERS = 256
MODES = 16
SEQ_LEN = 16384
SHARDS = 64
ROWS = 256
GROUPS = 4
F32 = jnp.float32
BF16 = jnp.bfloat16
LANES = 128
STEPS = 32
WORKERS = 16
SUBS = 8
TILES = 8
ACROSS = (((1,), (1,)), ((), ()))


def iota(shape, dim):
    return lax.broadcasted_iota(jnp.int32, shape, dim)


def identity(size):
    return (iota((size, size), 0) == iota((size, size), 1)).astype(BF16)


def reversal(size):
    row, col = iota((size, size), 0), iota((size, size), 1)
    return ((row + col == size) | ((row == 0) & (col == 0))).astype(BF16)


def load_signals(q_ref, k_ref, v_ref, o_ref, sig_ref):
    for tile in range(TILES):
        lanes = pl.ds(tile * LANES, LANES)
        conv_in = (k_ref[:, lanes].astype(F32) * v_ref[:, lanes].astype(F32)).astype(BF16)
        mid_grad = (o_ref[:, lanes].astype(F32) * q_ref[:, lanes].astype(F32)).astype(BF16)
        sig_ref[0, tile] = conv_in.astype(F32)
        sig_ref[1, tile] = mid_grad.astype(F32)


def pack_chunk(chunk, sig_ref, spread_ref, pack_ref):
    eye = identity(LANES)
    rev = reversal(LANES)
    for group in range(GROUPS):
        tile = 2 * group + chunk
        for sig in range(2):
            for half in range(2):
                block = sig_ref[sig, tile, half * LANES:(half + 1) * LANES, :].astype(BF16)
                if sig == 0:
                    block = jnp.dot(rev, block, preferred_element_type=F32).astype(BF16)
                turned = lax.dot_general(eye, block, ACROSS, preferred_element_type=F32)
                for low in range(2):
                    place = sig * 8 + low * 4 + group
                    spread_ref[half, pl.ds(place, SHARDS, stride=16), :] = turned[
                        low * SHARDS:(low + 1) * SHARDS
                    ]
    for half in range(2):
        pack_ref[chunk, :, half * LANES:(half + 1) * LANES] = spread_ref[half].astype(BF16)


def make_decays(rates_ref, weights_ref, base_ref, gain_ref, leave_ref, hop_ref):
    sub = iota((MODES, SUBS, LANES), 1)
    for side in range(2):
        lanes = slice(side * LANES, (side + 1) * LANES)
        rate = jnp.broadcast_to(rates_ref[:, lanes][:, None, :], (MODES, SUBS, LANES))
        weight = jnp.broadcast_to(weights_ref[:, lanes][:, None, :], (MODES, SUBS, LANES))
        base_ref[side] = jnp.exp(-rate)
        gain_ref[side] = weight * jnp.sqrt(rate)
        for sig in range(2):
            runs = SUBS - 1 - sub if sig == 0 else sub
            leave_ref[sig, side] = jnp.exp(-rate * (runs.astype(F32) * float(STEPS)))
            for at, hop in enumerate((1, 2, 4)):
                left = sub >= hop if sig == 0 else sub < SUBS - hop
                hop_ref[sig, side, at] = jnp.where(left, jnp.exp(-rate * float(STEPS * hop)), 0.0)


def block_states(sig_ref, base_ref, leave_ref, ends_ref, state_ref, state_out):
    def one_group(group, _):
        for side in range(2):
            tile = 2 * group + side
            base = base_ref[side]
            for sig in range(2):
                acc = None
                for step in range(STEPS):
                    place = step if sig == 0 else STEPS - 1 - step
                    row = sig_ref[sig, tile, pl.ds(place, SUBS, stride=STEPS), :]
                    wide = jnp.broadcast_to(row[None], (MODES, SUBS, LANES))
                    acc = wide if acc is None else base * acc + wide
                ends_ref[sig, tile] = acc
                start = pl.multiple_of((sig * TILES + tile) * MODES, MODES)
                state_ref[pl.ds(start, MODES), :] = jnp.sum(acc * leave_ref[sig, side], axis=1)
        return _
    lax.fori_loop(0, GROUPS, one_group, 0)
    for mode in range(MODES):
        state_out[mode] = state_ref[pl.ds(mode, 2 * TILES, stride=MODES), :].astype(BF16)


def owner_scan(decay, got_ref, first, enter_ref):
    fore, back = first
    for at in range(WORKERS):
        far = WORKERS - 1 - at
        if enter_ref is not None:
            enter_ref[at, :TILES, :] = fore
            enter_ref[far, TILES:, :] = back
        fore = decay * fore + got_ref[at, :, :].astype(F32)[:TILES]
        back = decay * back + got_ref[far, :, :].astype(F32)[TILES:]
    return fore, back


def run_recurrence(sig_ref, base_ref, gain_ref, hop_ref, ends_ref, enter_ref, long_ref):
    sub = iota((MODES, SUBS, LANES), 1)

    def one_group(group, _):
        for side in range(2):
            tile = 2 * group + side
            base, gain = base_ref[side], gain_ref[side]
            for sig in range(2):
                first = jnp.broadcast_to(enter_ref[sig * TILES + tile][:, None, :], (MODES, SUBS, LANES))
                ends = ends_ref[sig, tile]
                edge, turn = (0, 1) if sig == 0 else (SUBS - 1, SUBS - 1)
                held = jnp.where(sub == edge, first, pltpu.roll(ends, turn, 1))
                for at, hop in enumerate((1, 2, 4)):
                    moved = pltpu.roll(held, hop if sig == 0 else SUBS - hop, 1)
                    held = held + hop_ref[sig, side, at] * moved
                for step in range(STEPS):
                    place = step if sig == 0 else STEPS - 1 - step
                    where = pl.ds(place, SUBS, stride=STEPS)
                    row = sig_ref[sig, tile, where, :]
                    held = base * held + jnp.broadcast_to(row[None], (MODES, SUBS, LANES))
                    terms = gain * held
                    for width in (8, 4, 2, 1):
                        terms = terms[:width] + terms[width:]
                    long_ref[sig, tile, where, :] = terms[0]
        return _
    lax.fori_loop(0, GROUPS, one_group, 0)


def finish_outputs(q_ref, k_ref, v_ref, skip_ref, sig_ref, long_ref, layer_ref, kgrad_ref, vgrad_ref):
    for tile in range(TILES):
        lanes = pl.ds(tile * LANES, LANES)
        skip = skip_ref[:, lanes]
        layer = long_ref[0, tile] + skip * sig_ref[0, tile]
        layer_ref[:, lanes] = (q_ref[:, lanes].astype(F32) * layer).astype(BF16)
        total = long_ref[1, tile] + skip * sig_ref[1, tile]
        kgrad_ref[:, lanes] = (total * v_ref[:, lanes].astype(F32)).astype(BF16)
        vgrad_ref[:, lanes] = (total * k_ref[:, lanes].astype(F32)).astype(BF16)


PAD = ROWS
WINDOW = 528
LONG = 4


def correlate_filter(low, rows_ref, slide_ref, slid_ref, grad_ref, turn_ref, keep_ref, sums_ref):
    for half in range(2):
        lanes = slice(half * LANES, (half + 1) * LANES)
        for group in range(GROUPS):
            conv_rows = rows_ref[half, pl.ds(low * 4 + group, SHARDS, stride=16), :]
            for early in range(4):
                slide_ref[early, half, pl.ds(PAD + group + 4 * early, SHARDS, stride=4), :] = conv_rows
            grad_ref[half, pl.ds(group, SHARDS, stride=4), :] = rows_ref[
                half, pl.ds(8 + low * 4 + group, SHARDS, stride=16), :
            ]
        for early in range(4):
            slid_ref[early, :, lanes] = slide_ref[early, half, :2 * ROWS, :].astype(BF16)
        turn_ref[lanes, :] = lax.dot_general(
            identity(LANES), grad_ref[half].astype(BF16), ACROSS, preferred_element_type=F32
        ).astype(BF16)

    row, lane = iota((LANES, LANES), 0), iota((LANES, LANES), 1)
    causal = (lane == 0) | (row + lane >= LANES)
    turn = turn_ref[...]
    keep_ref[...] = jnp.zeros_like(keep_ref)

    def sheared(block):
        block = pltpu.roll(block, 0, 1, stride=1, stride_axis=0)
        return jnp.sum(block.reshape(LANES // SUBS, SUBS, LANES), axis=0)

    def some_lags(at, _):
        corner, later = keep_ref[0], keep_ref[1]
        for inner in range(LONG):
            far = SHARDS // 4 - 1 - (at * LONG + inner)
            for early in (3, 2, 1, 0):
                start = pl.multiple_of(PAD - 16 * far, 16)
                window = slid_ref[early, pl.ds(start, ROWS), :]
                prod = jnp.dot(turn, window, preferred_element_type=F32)
                odd = prod[LANES:, :LANES] + corner
                even = prod[:LANES, :LANES] + prod[LANES:, LANES:]
                place = pl.multiple_of((4 * far + early) * 2 * SUBS, 2 * SUBS)
                sums_ref[pl.ds(place, SUBS), :] = sheared(jnp.where(causal, even, odd))
                sums_ref[pl.ds(place + SUBS, SUBS), :] = sheared(jnp.where(causal, odd, later))
                corner, later = prod[:LANES, LANES:], even
        keep_ref[0], keep_ref[1] = corner, later
        return _
    lax.fori_loop(0, SHARDS // 4 // LONG, some_lags, 0)

    out = []
    for part in range(2):
        total = sums_ref[pl.ds(part * SUBS, SHARDS, stride=2 * SUBS), :]
        for sub in range(1, SUBS):
            total = total + sums_ref[pl.ds(part * SUBS + sub, SHARDS, stride=2 * SUBS), :]
        out.append(total)
    return jnp.concatenate(out, axis=0)


def seq_copy(src, dst, send, recv, to):
    return pltpu.make_async_remote_copy(
        src_ref=src, dst_ref=dst, send_sem=send, recv_sem=recv,
        device_id={"seq": to}, device_id_type=pl.DeviceIdType.MESH,
    )


def settle(ref, sem):
    pltpu.make_async_copy(ref, ref, sem).wait()


def layer_kernel(q_ref, k_ref, v_ref, o_ref, rates_ref, weights_ref, skip_ref,
                 layer_ref, kgrad_ref, vgrad_ref, taps_ref,
                 sig_ref, spread_ref, pack_ref, land_ref, base_ref, gain_ref, leave_ref, hop_ref, ends_ref,
                 state_ref, left_ref, got_ref, whole_ref, wholes_ref, enter_ref, given_ref, entered_ref, first_ref,
                 long_ref, rows_ref, slide_ref, slid_ref, grad_ref, turn_ref, keep_ref, sums_ref,
                 share_ref, sent_ref, came_ref, final_ref, home_ref, send_sem, recv_sem, own_sem):
    seq, chan = lax.axis_index("seq"), lax.axis_index("chan")
    row, worker = lax.div(seq, WORKERS), lax.rem(seq, WORKERS)
    barrier = pltpu.get_barrier_semaphore()

    def greet(step, _):
        pl.semaphore_signal(barrier, inc=1, device_id={"seq": lax.rem(seq + step, SHARDS)}, device_id_type=pl.DeviceIdType.MESH)
        return _
    lax.fori_loop(1, SHARDS, greet, 0)
    for step in range(1, 4):
        pl.semaphore_signal(barrier, inc=1, device_id={"chan": lax.rem(chan + step, 4)}, device_id_type=pl.DeviceIdType.MESH)

    load_signals(q_ref, k_ref, v_ref, o_ref, sig_ref)

    own_copies = []

    def send_chunk(chunk):
        mine = pl.ds(pl.multiple_of(seq * 16, 16), 16)
        own = pltpu.make_async_copy(pack_ref.at[chunk, mine], land_ref.at[chunk, mine], own_sem.at[chunk])
        own.start()
        own_copies.append(own)

        def one(step, _):
            to = lax.rem(seq + step, SHARDS)
            seq_copy(
                pack_ref.at[chunk, pl.ds(pl.multiple_of(to * 16, 16), 16)], land_ref.at[chunk, mine],
                send_sem.at[chunk], recv_sem.at[chunk], to,
            ).start()
            return _
        lax.fori_loop(1, SHARDS, one, 0)

    pack_chunk(0, sig_ref, spread_ref, pack_ref)
    pl.semaphore_wait(barrier, SHARDS - 1 + 3)
    send_chunk(0)
    pack_chunk(1, sig_ref, spread_ref, pack_ref)
    send_chunk(1)

    make_decays(rates_ref, weights_ref, base_ref, gain_ref, leave_ref, hop_ref)
    block_states(sig_ref, base_ref, leave_ref, ends_ref, state_ref, left_ref)

    def to_row(source, target, sem):
        own = pltpu.make_async_copy(source.at[worker], target.at[worker], own_sem.at[sem])
        own.start()

        def one(step, _):
            to = lax.rem(worker + step, WORKERS)
            seq_copy(source.at[to], target.at[worker], send_sem.at[sem], recv_sem.at[sem], row * WORKERS + to).start()
            return _
        lax.fori_loop(1, WORKERS, one, 0)
        return own

    def settle_row(source, target, sem, own):
        own.wait()
        settle(source.at[pl.ds(0, WORKERS - 1)], send_sem.at[sem])
        settle(target.at[pl.ds(0, WORKERS - 1)], recv_sem.at[sem])

    own = to_row(left_ref, got_ref, 2)
    slide_ref[...] = jnp.zeros_like(slide_ref)
    settle_row(left_ref, got_ref, 2, own)

    tile_row = iota((TILES, LANES), 0)
    mode_rates = rates_ref[pl.ds(worker, 1), :]
    rate = jnp.where(
        lax.rem(tile_row, 2) == 0,
        jnp.broadcast_to(mode_rates[:, :LANES], (TILES, LANES)),
        jnp.broadcast_to(mode_rates[:, LANES:], (TILES, LANES)),
    )
    decay = jnp.exp(-float(ROWS) * rate)
    zero = jnp.zeros((TILES, LANES), F32)
    fore, back = owner_scan(decay, got_ref, (zero, zero), None)
    whole_ref[:TILES] = fore
    whole_ref[TILES:] = back
    for step in range(1, 4):
        to = lax.rem(row + step, 4)
        seq_copy(whole_ref, wholes_ref.at[row], send_sem.at[3], recv_sem.at[3], to * WORKERS + worker).start()
    wholes_ref[row] = whole_ref[...]
    for step in range(1, 4):
        settle(whole_ref, send_sem.at[3])
    settle(wholes_ref.at[pl.ds(0, 3)], recv_sem.at[3])
    fore, back = zero, zero
    for other in range(4):
        ahead = (row - 1 - other).astype(F32)
        behind = (other - 1 - row).astype(F32)
        length = float(ROWS * WORKERS)
        fore = fore + jnp.where(
            ahead >= 0.0, jnp.exp(-rate * (length * jnp.maximum(ahead, 0.0))), 0.0
        ) * wholes_ref[other, :TILES, :]
        back = back + jnp.where(
            behind >= 0.0, jnp.exp(-rate * (length * jnp.maximum(behind, 0.0))), 0.0
        ) * wholes_ref[other, TILES:, :]
    owner_scan(decay, got_ref, (fore, back), enter_ref)
    given_ref[...] = enter_ref[...].astype(BF16)
    own = to_row(given_ref, entered_ref, 4)

    def correlate_chunk(chunk):
        own_copies[chunk].wait()
        settle(pack_ref.at[chunk, pl.ds(0, (SHARDS - 1) * 16)], send_sem.at[chunk])
        settle(land_ref.at[chunk, pl.ds(0, (SHARDS - 1) * 16)], recv_sem.at[chunk])
        for half in range(2):
            rows_ref[half] = land_ref[chunk, :, half * LANES:(half + 1) * LANES].astype(F32)
        for low in range(2):
            share = correlate_filter(low, rows_ref, slide_ref, slid_ref, grad_ref, turn_ref, keep_ref, sums_ref)
            share_ref[2 * chunk + low] = share
            sent_ref[2 * chunk + low] = share.astype(BF16)

    correlate_chunk(0)

    settle_row(given_ref, entered_ref, 4, own)
    for mode in range(MODES):
        rows = entered_ref[mode].astype(F32)
        enter_ref[mode] = rows
    state_all = enter_ref[...].reshape(MODES * MODES, LANES)
    state_ref[...] = state_all
    for place in range(2 * TILES):
        first_ref[place] = state_ref[pl.ds(place, MODES, stride=2 * TILES), :]
    run_recurrence(sig_ref, base_ref, gain_ref, hop_ref, ends_ref, first_ref, long_ref)
    finish_outputs(q_ref, k_ref, v_ref, skip_ref, sig_ref, long_ref, layer_ref, kgrad_ref, vgrad_ref)

    correlate_chunk(1)

    for step in range(1, 4):
        to = lax.rem(chan + step, 4)
        pltpu.make_async_remote_copy(
            src_ref=sent_ref.at[to], dst_ref=came_ref.at[chan], send_sem=send_sem.at[5], recv_sem=recv_sem.at[5],
            device_id={"chan": to}, device_id_type=pl.DeviceIdType.MESH,
        ).start()
    settle(sent_ref.at[pl.ds(0, 3)], send_sem.at[5])
    settle(came_ref.at[pl.ds(0, 3)], recv_sem.at[5])
    came_ref[chan] = jnp.zeros((LANES, LANES), BF16)
    taps = share_ref[chan]
    for other in range(4):
        taps = taps + came_ref[other].astype(F32)
    for part in range(2):
        final_ref[:, part, :] = taps[part * SHARDS:(part + 1) * SHARDS]
    own = pltpu.make_async_copy(final_ref.at[seq], home_ref.at[seq], own_sem.at[5])
    own.start()

    def last(step, _):
        to = lax.rem(seq + step, SHARDS)
        seq_copy(final_ref.at[to], home_ref.at[seq], send_sem.at[6], recv_sem.at[6], to).start()
        return _
    lax.fori_loop(1, SHARDS, last, 0)
    own.wait()
    settle(final_ref.at[pl.ds(0, SHARDS - 1)], send_sem.at[6])
    settle(home_ref.at[pl.ds(0, SHARDS - 1)], recv_sem.at[6])
    scale = 1.0 / math.sqrt(SEQ_LEN * (CHANNELS // FILTERS))
    for part in range(2):
        taps_ref[:, part * LANES:(part + 1) * LANES] = home_ref[:, part, :] * scale


SCRATCH = [
    pltpu.VMEM((2, TILES, ROWS, LANES), F32),
    pltpu.VMEM((2, SHARDS * 16, LANES), F32),
    pltpu.VMEM((2, SHARDS * 16, ROWS), BF16),
    pltpu.VMEM((2, SHARDS * 16, ROWS), BF16),
    pltpu.VMEM((2, MODES, SUBS, LANES), F32),
    pltpu.VMEM((2, MODES, SUBS, LANES), F32),
    pltpu.VMEM((2, 2, MODES, SUBS, LANES), F32),
    pltpu.VMEM((2, 2, 3, MODES, SUBS, LANES), F32),
    pltpu.VMEM((2, TILES, MODES, SUBS, LANES), F32),
    pltpu.VMEM((2 * TILES * MODES, LANES), F32),
    pltpu.VMEM((WORKERS, 2 * TILES, LANES), BF16),
    pltpu.VMEM((WORKERS, 2 * TILES, LANES), BF16),
    pltpu.VMEM((2 * TILES, LANES), F32),
    pltpu.VMEM((4, 2 * TILES, LANES), F32),
    pltpu.VMEM((WORKERS, 2 * TILES, LANES), F32),
    pltpu.VMEM((WORKERS, 2 * TILES, LANES), BF16),
    pltpu.VMEM((WORKERS, 2 * TILES, LANES), BF16),
    pltpu.VMEM((2 * TILES, MODES, LANES), F32),
    pltpu.VMEM((2, TILES, ROWS, LANES), F32),
    pltpu.VMEM((2, SHARDS * 16, LANES), F32),
    pltpu.VMEM((4, 2, WINDOW, LANES), F32),
    pltpu.VMEM((4, 2 * ROWS, ROWS), BF16),
    pltpu.VMEM((2, ROWS, LANES), F32),
    pltpu.VMEM((ROWS, ROWS), BF16),
    pltpu.VMEM((2, LANES, LANES), F32),
    pltpu.VMEM((SHARDS * 2 * SUBS, LANES), F32),
    pltpu.VMEM((4, LANES, LANES), F32),
    pltpu.VMEM((4, LANES, LANES), BF16),
    pltpu.VMEM((4, LANES, LANES), BF16),
    pltpu.VMEM((SHARDS, 2, LANES), F32),
    pltpu.VMEM((SHARDS, 2, LANES), F32),
    pltpu.SemaphoreType.DMA((7,)),
    pltpu.SemaphoreType.DMA((7,)),
    pltpu.SemaphoreType.DMA((7,)),
]
VMEM = pl.BlockSpec(memory_space=pltpu.VMEM)


def per_device(query_proj, key_proj, value_proj, out_grad, residues, decay_rate, skip_gain):
    sds = jax.ShapeDtypeStruct
    layer, kgrad, vgrad, taps = pl.pallas_call(
        layer_kernel,
        out_shape=(sds((ROWS, 1024), BF16),) * 3 + (sds((SHARDS, ROWS), F32),),
        in_specs=[VMEM] * 7,
        out_specs=(VMEM,) * 4,
        scratch_shapes=SCRATCH,
        compiler_params=pltpu.CompilerParams(
            vmem_limit_bytes=56 * 2**20, collective_id=0, has_side_effects=True
        ),
    )(query_proj, key_proj, value_proj, out_grad, decay_rate.T, residues.T, skip_gain[None, :])
    return (layer, kgrad, vgrad, taps.T)


def solution(mesh):
    wide = P("seq", "chan")
    return jax.shard_map(
        per_device,
        mesh=mesh,
        in_specs=(wide, wide, wide, wide, P(), P(), P("chan")),
        out_specs=(wide, wide, wide, wide),
        check_vma=False,
    )
```

time: 161 us -> 85 us (0.53)
  blocking collectives: 41.5 us -> 0 us
  starting transfers between devices: 27 us -> 0 us
  waiting for transfers between devices: 13.2 us -> 0 us
  Pallas kernels: 71 us -> 79.5 us
    all_to_all x1 -> x0, blocking collectives: 41.5 us -> none  [per_device(): lax.all_to_all(pack.reshape(2, SHARDS, 16, ROWS), 'seq', split_axis=1, co...]
    all_to_all x4 -> x0, starting transfers between devices: 27 us -> none  [the longest x1 11.9 us: per_device(): lax.all_to_all(enter, 'seq', split_axis=0, concat_axis=0, tiled=True)]
    all_to_all x4 -> x0, waiting for transfers between devices: 13.2 us -> none  [the longest x1 9.63 us: per_device(): lax.all_to_all(enter, 'seq', split_axis=0, concat_axis=0, tiled=True)]
    pallas_call x4 -> x1, Pallas kernels: 71 us -> 79.5 us  [per_device(): pl.pallas_call(layer_kernel, out_shape=(sds((ROWS, 1024), BF16),) * 3 + (...]
    unnamed x7 -> x10, local copies, waits for them, and re-layouts: 2.01 us -> 4.65 us
  transfers between devices with their start and end apart: 4 -> 0, of which waited for: 2 -> 0; matrix products, arithmetic and copies ran while one was open for 1% -> 0% of each run, Pallas kernels for 39% -> 0%
where the time goes in v2:
time: 85 us; the launch traced here: 84.8 us
  Pallas kernels  79.5 us (94%)
  local copies, waits for them, and re-layouts  4.65 us (5%)
    pallas_call x1, Pallas kernels, per_device(): pl.pallas_call(layer_kernel, out_shape=(sds((ROWS, 1024), BF16),) * 3 + (...  79.5 us
    unnamed x10, local copies, waits for them, and re-layouts  4.65 us

profile of v2, /device:TPU:1, one launch (start us, length us, event | category | flops | bytes accessed | tf_op | source)
XLA Modules:
  0.0 84.8 jit_solution(229077690710201120)
XLA Ops:
  0.6 79.5 %shard_map.102 = (bf16[256,1024]{1,0:T(8,128)(2,1)}, bf16[256,1024]{1,0:T(8,128)(2,1)}, bf16[256,1024]{1,0:T(8,128)(2,1)}, f32[64,256]{1,0:T(8,128)}) custom-call(bf16[256,1024]{1,0:T(8,128)(2,1)} %q_ref.1, bf16[256,1024]{1,0:T(8,128)(2,1)} %k_ref.1, bf16[256,1024]{1,0:T(8,128)(2,1)} %v_ref.1, bf16[256,1024]{1,0:T(8,128)(2,1)} %o_ref.1, f32[16,256]{1,0:T(8,128)} %bitcast.5, ...), custom_call_target="tpu_custom_call" | custom-call | tf_op jit(solution)/shard_map/pallas_call | solution.py:421
  80.1 0.0 copy-start.1
  80.1 1.9 %copy.15 = bf16[256,1024]{1,0:T(8,128)(2,1)} copy(bf16[256,1024]{1,0:T(8,128)(2,1)} %get-tuple-element.16) | data formatting | bytes 1048576
  82.1 0.0 copy-done.1
  82.1 0.0 copy-start
  82.1 0.8 copy.16
  82.9 0.4 copy-done
  83.3 0.0 copy-start.2
  83.3 0.8 copy.17
  84.1 0.1 copy-done.2
  84.2 0.6 copy.18
Async XLA Ops:
  80.1 1.9 %copy-start.1 = (bf16[256,1024]{1,0:T(8,128)(2,1)S(1)}, bf16[256,1024]{1,0:T(8,128)(2,1)}, u32[]{:S(2)}) copy-start(bf16[256,1024]{1,0:T(8,128)(2,1)} %get-tuple-element.17) | copy-start | bytes 1572868
  82.1 1.2 %copy-start = (bf16[256,1024]{1,0:T(8,128)(2,1)S(1)}, bf16[256,1024]{1,0:T(8,128)(2,1)}, u32[]{:S(2)}) copy-start(bf16[256,1024]{1,0:T(8,128)(2,1)} %get-tuple-element.18) | copy-start | bytes 1572868
  83.3 0.9 %copy-start.2 = (f32[64,256]{1,0:T(8,128)S(1)}, f32[64,256]{1,0:T(8,128)}, u32[]{:S(2)}) copy-start(f32[64,256]{1,0:T(8,128)} %get-tuple-element.11) | copy-start | bytes 196612

commit v3 on v2

--- a/solution.py
+++ b/solution.py
@@ -46,11 +46,11 @@
         sig_ref[1, tile] = mid_grad.astype(F32)
 
 
-def pack_chunk(chunk, sig_ref, spread_ref, pack_ref):
+def pack_pair(pair, chan, sig_ref, spread_ref, pack_ref):
     eye = identity(LANES)
     rev = reversal(LANES)
     for group in range(GROUPS):
-        tile = 2 * group + chunk
+        tile = 2 * group + pair
         for sig in range(2):
             for half in range(2):
                 block = sig_ref[sig, tile, half * LANES:(half + 1) * LANES, :].astype(BF16)
@@ -58,12 +58,11 @@
                     block = jnp.dot(rev, block, preferred_element_type=F32).astype(BF16)
                 turned = lax.dot_general(eye, block, ACROSS, preferred_element_type=F32)
                 for low in range(2):
-                    place = sig * 8 + low * 4 + group
-                    spread_ref[half, pl.ds(place, SHARDS, stride=16), :] = turned[
+                    spread_ref[low, pl.ds(half * 8 + sig * 4 + group, SHARDS, stride=16), :] = turned[
                         low * SHARDS:(low + 1) * SHARDS
                     ]
-    for half in range(2):
-        pack_ref[chunk, :, half * LANES:(half + 1) * LANES] = spread_ref[half].astype(BF16)
+    for low in range(2):
+        pack_ref[lax.rem(2 * pair + low + 3 - chan, 4)] = spread_ref[low].astype(BF16)
 
 
 def make_decays(rates_ref, weights_ref, base_ref, gain_ref, leave_ref, hop_ref):
@@ -155,52 +154,43 @@
 
 
 PAD = ROWS
-WINDOW = 528
-LONG = 4
-
-
-def correlate_filter(low, rows_ref, slide_ref, slid_ref, grad_ref, turn_ref, keep_ref, sums_ref):
+
+
+def correlate_filter(land_ref, rows_ref, slide_ref, slid_ref, grad_ref, turn_ref, sums_ref):
+    rows_ref[...] = land_ref[...].astype(F32)
     for half in range(2):
         lanes = slice(half * LANES, (half + 1) * LANES)
         for group in range(GROUPS):
-            conv_rows = rows_ref[half, pl.ds(low * 4 + group, SHARDS, stride=16), :]
+            conv_rows = rows_ref[pl.ds(half * 8 + group, SHARDS, stride=16), :]
             for early in range(4):
-                slide_ref[early, half, pl.ds(PAD + group + 4 * early, SHARDS, stride=4), :] = conv_rows
+                slide_ref[early, half, pl.ds(group + 4 * early, SHARDS, stride=4), :] = conv_rows
             grad_ref[half, pl.ds(group, SHARDS, stride=4), :] = rows_ref[
-                half, pl.ds(8 + low * 4 + group, SHARDS, stride=16), :
+                pl.ds(half * 8 + 4 + group, SHARDS, stride=16), :
             ]
         for early in range(4):
-            slid_ref[early, :, lanes] = slide_ref[early, half, :2 * ROWS, :].astype(BF16)
+            slid_ref[early, PAD:, lanes] = slide_ref[early, half, :ROWS, :].astype(BF16)
         turn_ref[lanes, :] = lax.dot_general(
             identity(LANES), grad_ref[half].astype(BF16), ACROSS, preferred_element_type=F32
         ).astype(BF16)
 
     row, lane = iota((LANES, LANES), 0), iota((LANES, LANES), 1)
     causal = (lane == 0) | (row + lane >= LANES)
-    turn = turn_ref[...]
-    keep_ref[...] = jnp.zeros_like(keep_ref)
 
     def sheared(block):
         block = pltpu.roll(block, 0, 1, stride=1, stride_axis=0)
         return jnp.sum(block.reshape(LANES // SUBS, SUBS, LANES), axis=0)
 
-    def some_lags(at, _):
-        corner, later = keep_ref[0], keep_ref[1]
-        for inner in range(LONG):
-            far = SHARDS // 4 - 1 - (at * LONG + inner)
-            for early in (3, 2, 1, 0):
-                start = pl.multiple_of(PAD - 16 * far, 16)
-                window = slid_ref[early, pl.ds(start, ROWS), :]
-                prod = jnp.dot(turn, window, preferred_element_type=F32)
-                odd = prod[LANES:, :LANES] + corner
-                even = prod[:LANES, :LANES] + prod[LANES:, LANES:]
-                place = pl.multiple_of((4 * far + early) * 2 * SUBS, 2 * SUBS)
-                sums_ref[pl.ds(place, SUBS), :] = sheared(jnp.where(causal, even, odd))
-                sums_ref[pl.ds(place + SUBS, SUBS), :] = sheared(jnp.where(causal, odd, later))
-                corner, later = prod[:LANES, LANES:], even
-        keep_ref[0], keep_ref[1] = corner, later
-        return _
-    lax.fori_loop(0, SHARDS // 4 // LONG, some_lags, 0)
+    corner = later = jnp.zeros((LANES, LANES), F32)
+    for block_lag in range(SHARDS - 1, -1, -1):
+        start = PAD - 16 * (block_lag // 4)
+        window = slid_ref[block_lag % 4, start:start + ROWS, :]
+        prod = jnp.dot(turn_ref[...], window, preferred_element_type=F32)
+        odd = prod[LANES:, :LANES] + corner
+        even = prod[:LANES, :LANES] + prod[LANES:, LANES:]
+        place = block_lag * 2 * SUBS
+        sums_ref[place:place + SUBS, :] = sheared(jnp.where(causal, even, odd))
+        sums_ref[place + SUBS:place + 2 * SUBS, :] = sheared(jnp.where(causal, odd, later))
+        corner, later = prod[:LANES, LANES:], even
 
     out = []
     for part in range(2):
@@ -222,12 +212,15 @@
     pltpu.make_async_copy(ref, ref, sem).wait()
 
 
+STATES, TOTALS, ENTERING, SHARE, FINAL = 4, 5, 6, 7, 10
+
+
 def layer_kernel(q_ref, k_ref, v_ref, o_ref, rates_ref, weights_ref, skip_ref,
                  layer_ref, kgrad_ref, vgrad_ref, taps_ref,
                  sig_ref, spread_ref, pack_ref, land_ref, base_ref, gain_ref, leave_ref, hop_ref, ends_ref,
                  state_ref, left_ref, got_ref, whole_ref, wholes_ref, enter_ref, given_ref, entered_ref, first_ref,
-                 long_ref, rows_ref, slide_ref, slid_ref, grad_ref, turn_ref, keep_ref, sums_ref,
-                 share_ref, sent_ref, came_ref, final_ref, home_ref, send_sem, recv_sem, own_sem):
+                 long_ref, rows_ref, slide_ref, slid_ref, grad_ref, turn_ref, sums_ref,
+                 sent_ref, came_ref, final_ref, home_ref, send_sem, recv_sem, own_sem):
     seq, chan = lax.axis_index("seq"), lax.axis_index("chan")
     row, worker = lax.div(seq, WORKERS), lax.rem(seq, WORKERS)
     barrier = pltpu.get_barrier_semaphore()
@@ -239,33 +232,22 @@
     for step in range(1, 4):
         pl.semaphore_signal(barrier, inc=1, device_id={"chan": lax.rem(chan + step, 4)}, device_id_type=pl.DeviceIdType.MESH)
 
-    load_signals(q_ref, k_ref, v_ref, o_ref, sig_ref)
-
-    own_copies = []
-
-    def send_chunk(chunk):
+    own_copies = {}
+
+    def send_filter(place):
         mine = pl.ds(pl.multiple_of(seq * 16, 16), 16)
-        own = pltpu.make_async_copy(pack_ref.at[chunk, mine], land_ref.at[chunk, mine], own_sem.at[chunk])
+        own = pltpu.make_async_copy(pack_ref.at[place, mine], land_ref.at[place, mine], own_sem.at[place])
         own.start()
-        own_copies.append(own)
+        own_copies[place] = own
 
         def one(step, _):
             to = lax.rem(seq + step, SHARDS)
             seq_copy(
-                pack_ref.at[chunk, pl.ds(pl.multiple_of(to * 16, 16), 16)], land_ref.at[chunk, mine],
-                send_sem.at[chunk], recv_sem.at[chunk], to,
+                pack_ref.at[place, pl.ds(pl.multiple_of(to * 16, 16), 16)], land_ref.at[place, mine],
+                send_sem.at[place], recv_sem.at[place], to,
             ).start()
             return _
         lax.fori_loop(1, SHARDS, one, 0)
-
-    pack_chunk(0, sig_ref, spread_ref, pack_ref)
-    pl.semaphore_wait(barrier, SHARDS - 1 + 3)
-    send_chunk(0)
-    pack_chunk(1, sig_ref, spread_ref, pack_ref)
-    send_chunk(1)
-
-    make_decays(rates_ref, weights_ref, base_ref, gain_ref, leave_ref, hop_ref)
-    block_states(sig_ref, base_ref, leave_ref, ends_ref, state_ref, left_ref)
 
     def to_row(source, target, sem):
         own = pltpu.make_async_copy(source.at[worker], target.at[worker], own_sem.at[sem])
@@ -283,10 +265,40 @@
         settle(source.at[pl.ds(0, WORKERS - 1)], send_sem.at[sem])
         settle(target.at[pl.ds(0, WORKERS - 1)], recv_sem.at[sem])
 
-    own = to_row(left_ref, got_ref, 2)
+    def correlate(place):
+        own_copies[place].wait()
+        settle(pack_ref.at[place, pl.ds(0, (SHARDS - 1) * 16)], send_sem.at[place])
+        settle(land_ref.at[place, pl.ds(0, (SHARDS - 1) * 16)], recv_sem.at[place])
+        return correlate_filter(
+            land_ref.at[place], rows_ref, slide_ref, slid_ref, grad_ref, turn_ref, sums_ref
+        )
+
+    def share_copy(place):
+        return pltpu.make_async_remote_copy(
+            src_ref=sent_ref.at[place], dst_ref=came_ref.at[place],
+            send_sem=send_sem.at[SHARE + place], recv_sem=recv_sem.at[SHARE + place],
+            device_id={"chan": lax.rem(chan + 1 + place, 4)}, device_id_type=pl.DeviceIdType.MESH,
+        )
+
+    def correlate_and_share(place):
+        sent_ref[place] = correlate(place).astype(BF16)
+        share_copy(place).start()
+
+    load_signals(q_ref, k_ref, v_ref, o_ref, sig_ref)
+    early_pair = lax.div(lax.rem(chan + 1, 4), 2)
+    pack_pair(early_pair, chan, sig_ref, spread_ref, pack_ref)
+    pl.semaphore_wait(barrier, SHARDS - 1 + 3)
+    send_filter(0)
+
+    make_decays(rates_ref, weights_ref, base_ref, gain_ref, leave_ref, hop_ref)
+    block_states(sig_ref, base_ref, leave_ref, ends_ref, state_ref, left_ref)
+    own_states = to_row(left_ref, got_ref, STATES)
+    pack_pair(1 - early_pair, chan, sig_ref, spread_ref, pack_ref)
+    send_filter(1)
     slide_ref[...] = jnp.zeros_like(slide_ref)
-    settle_row(left_ref, got_ref, 2, own)
-
+    slid_ref[:, :PAD, :] = jnp.zeros_like(slid_ref[:, :PAD, :])
+
+    settle_row(left_ref, got_ref, STATES, own_states)
     tile_row = iota((TILES, LANES), 0)
     mode_rates = rates_ref[pl.ds(worker, 1), :]
     rate = jnp.where(
@@ -301,11 +313,16 @@
     whole_ref[TILES:] = back
     for step in range(1, 4):
         to = lax.rem(row + step, 4)
-        seq_copy(whole_ref, wholes_ref.at[row], send_sem.at[3], recv_sem.at[3], to * WORKERS + worker).start()
+        seq_copy(
+            whole_ref, wholes_ref.at[row], send_sem.at[TOTALS], recv_sem.at[TOTALS], to * WORKERS + worker
+        ).start()
     wholes_ref[row] = whole_ref[...]
+
+    correlate_and_share(0)
+
     for step in range(1, 4):
-        settle(whole_ref, send_sem.at[3])
-    settle(wholes_ref.at[pl.ds(0, 3)], recv_sem.at[3])
+        settle(whole_ref, send_sem.at[TOTALS])
+    settle(wholes_ref.at[pl.ds(0, 3)], recv_sem.at[TOTALS])
     fore, back = zero, zero
     for other in range(4):
         ahead = (row - 1 - other).astype(F32)
@@ -319,59 +336,37 @@
         ) * wholes_ref[other, TILES:, :]
     owner_scan(decay, got_ref, (fore, back), enter_ref)
     given_ref[...] = enter_ref[...].astype(BF16)
-    own = to_row(given_ref, entered_ref, 4)
-
-    def correlate_chunk(chunk):
-        own_copies[chunk].wait()
-        settle(pack_ref.at[chunk, pl.ds(0, (SHARDS - 1) * 16)], send_sem.at[chunk])
-        settle(land_ref.at[chunk, pl.ds(0, (SHARDS - 1) * 16)], recv_sem.at[chunk])
-        for half in range(2):
-            rows_ref[half] = land_ref[chunk, :, half * LANES:(half + 1) * LANES].astype(F32)
-        for low in range(2):
-            share = correlate_filter(low, rows_ref, slide_ref, slid_ref, grad_ref, turn_ref, keep_ref, sums_ref)
-            share_ref[2 * chunk + low] = share
-            sent_ref[2 * chunk + low] = share.astype(BF16)
-
-    correlate_chunk(0)
-
-    settle_row(given_ref, entered_ref, 4, own)
-    for mode in range(MODES):
-        rows = entered_ref[mode].astype(F32)
-        enter_ref[mode] = rows
-    state_all = enter_ref[...].reshape(MODES * MODES, LANES)
-    state_ref[...] = state_all
+    own_entering = to_row(given_ref, entered_ref, ENTERING)
+    send_filter(2)
+
+    correlate_and_share(1)
+    send_filter(3)
+
+    settle_row(given_ref, entered_ref, ENTERING, own_entering)
+    state_ref[...] = entered_ref[...].astype(F32).reshape(MODES * MODES, LANES)
     for place in range(2 * TILES):
         first_ref[place] = state_ref[pl.ds(place, MODES, stride=2 * TILES), :]
     run_recurrence(sig_ref, base_ref, gain_ref, hop_ref, ends_ref, first_ref, long_ref)
     finish_outputs(q_ref, k_ref, v_ref, skip_ref, sig_ref, long_ref, layer_ref, kgrad_ref, vgrad_ref)
 
-    correlate_chunk(1)
-
-    for step in range(1, 4):
-        to = lax.rem(chan + step, 4)
-        pltpu.make_async_remote_copy(
-            src_ref=sent_ref.at[to], dst_ref=came_ref.at[chan], send_sem=send_sem.at[5], recv_sem=recv_sem.at[5],
-            device_id={"chan": to}, device_id_type=pl.DeviceIdType.MESH,
-        ).start()
-    settle(sent_ref.at[pl.ds(0, 3)], send_sem.at[5])
-    settle(came_ref.at[pl.ds(0, 3)], recv_sem.at[5])
-    came_ref[chan] = jnp.zeros((LANES, LANES), BF16)
-    taps = share_ref[chan]
-    for other in range(4):
-        taps = taps + came_ref[other].astype(F32)
+    correlate_and_share(2)
+    taps = correlate(3)
+    for place in range(3):
+        share_copy(place).wait()
+        taps = taps + came_ref[place].astype(F32)
     for part in range(2):
         final_ref[:, part, :] = taps[part * SHARDS:(part + 1) * SHARDS]
-    own = pltpu.make_async_copy(final_ref.at[seq], home_ref.at[seq], own_sem.at[5])
+    own = pltpu.make_async_copy(final_ref.at[seq], home_ref.at[seq], own_sem.at[FINAL])
     own.start()
 
     def last(step, _):
         to = lax.rem(seq + step, SHARDS)
-        seq_copy(final_ref.at[to], home_ref.at[seq], send_sem.at[6], recv_sem.at[6], to).start()
+        seq_copy(final_ref.at[to], home_ref.at[seq], send_sem.at[FINAL], recv_sem.at[FINAL], to).start()
         return _
     lax.fori_loop(1, SHARDS, last, 0)
     own.wait()
-    settle(final_ref.at[pl.ds(0, SHARDS - 1)], send_sem.at[6])
-    settle(home_ref.at[pl.ds(0, SHARDS - 1)], recv_sem.at[6])
+    settle(final_ref.at[pl.ds(0, SHARDS - 1)], send_sem.at[FINAL])
+    settle(home_ref.at[pl.ds(0, SHARDS - 1)], recv_sem.at[FINAL])
     scale = 1.0 / math.sqrt(SEQ_LEN * (CHANNELS // FILTERS))
     for part in range(2):
         taps_ref[:, part * LANES:(part + 1) * LANES] = home_ref[:, part, :] * scale
@@ -380,8 +375,8 @@
 SCRATCH = [
     pltpu.VMEM((2, TILES, ROWS, LANES), F32),
     pltpu.VMEM((2, SHARDS * 16, LANES), F32),
-    pltpu.VMEM((2, SHARDS * 16, ROWS), BF16),
-    pltpu.VMEM((2, SHARDS * 16, ROWS), BF16),
+    pltpu.VMEM((4, SHARDS * 16, LANES), BF16),
+    pltpu.VMEM((4, SHARDS * 16, LANES), BF16),
     pltpu.VMEM((2, MODES, SUBS, LANES), F32),
     pltpu.VMEM((2, MODES, SUBS, LANES), F32),
     pltpu.VMEM((2, 2, MODES, SUBS, LANES), F32),
@@ -397,21 +392,19 @@
     pltpu.VMEM((WORKERS, 2 * TILES, LANES), BF16),
     pltpu.VMEM((2 * TILES, MODES, LANES), F32),
     pltpu.VMEM((2, TILES, ROWS, LANES), F32),
-    pltpu.VMEM((2, SHARDS * 16, LANES), F32),
-    pltpu.VMEM((4, 2, WINDOW, LANES), F32),
+    pltpu.VMEM((SHARDS * 16, LANES), F32),
+    pltpu.VMEM((4, 2, ROWS + 16, LANES), F32),
     pltpu.VMEM((4, 2 * ROWS, ROWS), BF16),
     pltpu.VMEM((2, ROWS, LANES), F32),
     pltpu.VMEM((ROWS, ROWS), BF16),
-    pltpu.VMEM((2, LANES, LANES), F32),
     pltpu.VMEM((SHARDS * 2 * SUBS, LANES), F32),
-    pltpu.VMEM((4, LANES, LANES), F32),
-    pltpu.VMEM((4, LANES, LANES), BF16),
-    pltpu.VMEM((4, LANES, LANES), BF16),
+    pltpu.VMEM((3, LANES, LANES), BF16),
+    pltpu.VMEM((3, LANES, LANES), BF16),
     pltpu.VMEM((SHARDS, 2, LANES), F32),
     pltpu.VMEM((SHARDS, 2, LANES), F32),
-    pltpu.SemaphoreType.DMA((7,)),
-    pltpu.SemaphoreType.DMA((7,)),
-    pltpu.SemaphoreType.DMA((7,)),
+    pltpu.SemaphoreType.DMA((11,)),
+    pltpu.SemaphoreType.DMA((11,)),
+    pltpu.SemaphoreType.DMA((11,)),
 ]
 VMEM = pl.BlockSpec(memory_space=pltpu.VMEM)
 

time: 85 us -> 59.7 us (0.70)
  Pallas kernels: 79.5 us -> 54.2 us
    pallas_call x1, Pallas kernels: 79.5 us -> 54.2 us  [per_device(): pl.pallas_call(layer_kernel, out_shape=(sds((ROWS, 1024), BF16),) * 3 + (...]
where the time goes in v3:
time: 59.7 us; the launch traced here: 59.5 us
  Pallas kernels  54.2 us (91%)
  local copies, waits for them, and re-layouts  4.65 us (8%)
  between operations  0.65 us (1%)
    pallas_call x1, Pallas kernels, per_device(): pl.pallas_call(layer_kernel, out_shape=(sds((ROWS, 1024), BF16),) * 3 + (...  54.2 us
    unnamed x10, local copies, waits for them, and re-layouts  4.65 us

profile of v3, /device:TPU:1, one launch (start us, length us, event | category | flops | bytes accessed | tf_op | source)
XLA Modules:
  0.0 59.5 jit_solution(18016762759917212205)
XLA Ops:
  0.6 54.2 %shard_map.102 = (bf16[256,1024]{1,0:T(8,128)(2,1)}, bf16[256,1024]{1,0:T(8,128)(2,1)}, bf16[256,1024]{1,0:T(8,128)(2,1)}, f32[64,256]{1,0:T(8,128)}) custom-call(bf16[256,1024]{1,0:T(8,128)(2,1)} %q_ref.1, bf16[256,1024]{1,0:T(8,128)(2,1)} %k_ref.1, bf16[256,1024]{1,0:T(8,128)(2,1)} %v_ref.1, bf16[256,1024]{1,0:T(8,128)(2,1)} %o_ref.1, f32[16,256]{1,0:T(8,128)} %bitcast.5, ...), custom_call_target="tpu_custom_call" | custom-call | tf_op jit(solution)/shard_map/pallas_call | solution.py:414
  54.8 0.0 copy-start.1
  54.8 1.9 %copy.15 = bf16[256,1024]{1,0:T(8,128)(2,1)} copy(bf16[256,1024]{1,0:T(8,128)(2,1)} %get-tuple-element.16) | data formatting | bytes 1048576
  56.7 0.0 copy-done.1
  56.7 0.0 copy-start
  56.8 0.8 %copy.16 = bf16[256,1024]{1,0:T(8,128)(2,1)} copy(bf16[256,1024]{1,0:T(8,128)(2,1)S(1)} %copy-done.1) | data formatting | bytes 1048576
  57.5 0.4 copy-done
  58.0 0.0 copy-start.2
  58.0 0.8 %copy.17 = bf16[256,1024]{1,0:T(8,128)(2,1)} copy(bf16[256,1024]{1,0:T(8,128)(2,1)S(1)} %copy-done) | data formatting | bytes 1048576
  58.8 0.1 copy-done.2
  58.8 0.6 %copy.18 = f32[256,64]{0,1:T(8,128)} copy(f32[256,64]{0,1:T(8,128)S(1)} %bitcast.4) | data formatting | bytes 131072
Async XLA Ops:
  54.8 1.9 %copy-start.1 = (bf16[256,1024]{1,0:T(8,128)(2,1)S(1)}, bf16[256,1024]{1,0:T(8,128)(2,1)}, u32[]{:S(2)}) copy-start(bf16[256,1024]{1,0:T(8,128)(2,1)} %get-tuple-element.17) | copy-start | bytes 1572868
  56.7 1.2 %copy-start = (bf16[256,1024]{1,0:T(8,128)(2,1)S(1)}, bf16[256,1024]{1,0:T(8,128)(2,1)}, u32[]{:S(2)}) copy-start(bf16[256,1024]{1,0:T(8,128)(2,1)} %get-tuple-element.18) | copy-start | bytes 1572868
  58.0 0.9 %copy-start.2 = (f32[64,256]{1,0:T(8,128)S(1)}, f32[64,256]{1,0:T(8,128)}, u32[]{:S(2)}) copy-start(f32[64,256]{1,0:T(8,128)} %get-tuple-element.11) | copy-start | bytes 196612

commit v4 on v3

--- a/solution.py
+++ b/solution.py
@@ -37,13 +37,10 @@
     return ((row + col == size) | ((row == 0) & (col == 0))).astype(BF16)
 
 
-def load_signals(q_ref, k_ref, v_ref, o_ref, sig_ref):
-    for tile in range(TILES):
-        lanes = pl.ds(tile * LANES, LANES)
-        conv_in = (k_ref[:, lanes].astype(F32) * v_ref[:, lanes].astype(F32)).astype(BF16)
-        mid_grad = (o_ref[:, lanes].astype(F32) * q_ref[:, lanes].astype(F32)).astype(BF16)
-        sig_ref[0, tile] = conv_in.astype(F32)
-        sig_ref[1, tile] = mid_grad.astype(F32)
+def load_signals(tile, in_ref, sig_ref):
+    query, key, value, grad = (in_ref[at, tile].astype(F32) for at in range(4))
+    sig_ref[0, tile] = (key * value).astype(BF16).astype(F32)
+    sig_ref[1, tile] = (grad * query).astype(BF16).astype(F32)
 
 
 def pack_pair(pair, chan, sig_ref, spread_ref, pack_ref):
@@ -68,9 +65,9 @@
 def make_decays(rates_ref, weights_ref, base_ref, gain_ref, leave_ref, hop_ref):
     sub = iota((MODES, SUBS, LANES), 1)
     for side in range(2):
-        lanes = slice(side * LANES, (side + 1) * LANES)
-        rate = jnp.broadcast_to(rates_ref[:, lanes][:, None, :], (MODES, SUBS, LANES))
-        weight = jnp.broadcast_to(weights_ref[:, lanes][:, None, :], (MODES, SUBS, LANES))
+        rows = slice(side * MODES, (side + 1) * MODES)
+        rate = jnp.broadcast_to(rates_ref[rows, :][:, None, :], (MODES, SUBS, LANES))
+        weight = jnp.broadcast_to(weights_ref[rows, :][:, None, :], (MODES, SUBS, LANES))
         base_ref[side] = jnp.exp(-rate)
         gain_ref[side] = weight * jnp.sqrt(rate)
         for sig in range(2):
@@ -142,21 +139,22 @@
     lax.fori_loop(0, GROUPS, one_group, 0)
 
 
-def finish_outputs(q_ref, k_ref, v_ref, skip_ref, sig_ref, long_ref, layer_ref, kgrad_ref, vgrad_ref):
+def finish_outputs(in_ref, skip_ref, sig_ref, long_ref, layer_ref, kgrad_ref, vgrad_ref):
     for tile in range(TILES):
         lanes = pl.ds(tile * LANES, LANES)
-        skip = skip_ref[:, lanes]
+        skip = skip_ref[tile:tile + 1, :]
         layer = long_ref[0, tile] + skip * sig_ref[0, tile]
-        layer_ref[:, lanes] = (q_ref[:, lanes].astype(F32) * layer).astype(BF16)
+        layer_ref[:, lanes] = (in_ref[0, tile].astype(F32) * layer).astype(BF16)
         total = long_ref[1, tile] + skip * sig_ref[1, tile]
-        kgrad_ref[:, lanes] = (total * v_ref[:, lanes].astype(F32)).astype(BF16)
-        vgrad_ref[:, lanes] = (total * k_ref[:, lanes].astype(F32)).astype(BF16)
+        kgrad_ref[:, lanes] = (total * in_ref[2, tile].astype(F32)).astype(BF16)
+        vgrad_ref[:, lanes] = (total * in_ref[1, tile].astype(F32)).astype(BF16)
 
 
 PAD = ROWS
-
-
-def correlate_filter(land_ref, rows_ref, slide_ref, slid_ref, grad_ref, turn_ref, sums_ref):
+HALF = SHARDS // 2
+
+
+def prepare_filter(land_ref, rows_ref, slide_ref, slid_ref, grad_ref, turn_ref):
     rows_ref[...] = land_ref[...].astype(F32)
     for half in range(2):
         lanes = slice(half * LANES, (half + 1) * LANES)
@@ -173,6 +171,16 @@
             identity(LANES), grad_ref[half].astype(BF16), ACROSS, preferred_element_type=F32
         ).astype(BF16)
 
+
+def lag_product(block_lag, slid_ref, turn_ref):
+    start = PAD - 16 * (block_lag // 4)
+    if not isinstance(start, int):
+        start = pl.multiple_of(start, 16)
+    window = slid_ref[block_lag % 4, pl.ds(start, ROWS), :]
+    return jnp.dot(turn_ref[...], window, preferred_element_type=F32)
+
+
+def lag_rows(prod, corner, later):
     row, lane = iota((LANES, LANES), 0), iota((LANES, LANES), 1)
     causal = (lane == 0) | (row + lane >= LANES)
 
@@ -180,25 +188,34 @@
         block = pltpu.roll(block, 0, 1, stride=1, stride_axis=0)
         return jnp.sum(block.reshape(LANES // SUBS, SUBS, LANES), axis=0)
 
-    corner = later = jnp.zeros((LANES, LANES), F32)
-    for block_lag in range(SHARDS - 1, -1, -1):
-        start = PAD - 16 * (block_lag // 4)
-        window = slid_ref[block_lag % 4, start:start + ROWS, :]
-        prod = jnp.dot(turn_ref[...], window, preferred_element_type=F32)
-        odd = prod[LANES:, :LANES] + corner
-        even = prod[:LANES, :LANES] + prod[LANES:, LANES:]
+    odd = prod[LANES:, :LANES] + corner
+    even = prod[:LANES, :LANES] + prod[LANES:, LANES:]
+    pair = (sheared(jnp.where(causal, even, odd)), sheared(jnp.where(causal, odd, later)))
+    return pair, prod[:LANES, LANES:], even
+
+
+def correlate_lags(longest, shortest, carried, slid_ref, turn_ref, sums_ref):
+    corner, later = carried
+    for block_lag in range(longest, shortest - 1, -1):
+        pair, corner, later = lag_rows(lag_product(block_lag, slid_ref, turn_ref), corner, later)
         place = block_lag * 2 * SUBS
-        sums_ref[place:place + SUBS, :] = sheared(jnp.where(causal, even, odd))
-        sums_ref[place + SUBS:place + 2 * SUBS, :] = sheared(jnp.where(causal, odd, later))
-        corner, later = prod[:LANES, LANES:], even
+        sums_ref[place:place + SUBS, :] = pair[0]
+        sums_ref[place + SUBS:place + 2 * SUBS, :] = pair[1]
 
     out = []
+    count = longest - shortest + 1
     for part in range(2):
-        total = sums_ref[pl.ds(part * SUBS, SHARDS, stride=2 * SUBS), :]
-        for sub in range(1, SUBS):
-            total = total + sums_ref[pl.ds(part * SUBS + sub, SHARDS, stride=2 * SUBS), :]
+        total = None
+        for sub in range(SUBS):
+            start = (shortest * 2 + part) * SUBS + sub
+            rows = sums_ref[pl.ds(start, count, stride=2 * SUBS), :]
+            total = rows if total is None else total + rows
         out.append(total)
-    return jnp.concatenate(out, axis=0)
+    return out, (corner, later)
+
+
+def no_carry():
+    return (jnp.zeros((LANES, LANES), F32),) * 2
 
 
 def seq_copy(src, dst, send, recv, to):
@@ -215,14 +232,33 @@
 STATES, TOTALS, ENTERING, SHARE, FINAL = 4, 5, 6, 7, 10
 
 
-def layer_kernel(q_ref, k_ref, v_ref, o_ref, rates_ref, weights_ref, skip_ref,
+def layer_kernel(q_ref, k_ref, v_ref, o_ref, small_ref,
                  layer_ref, kgrad_ref, vgrad_ref, taps_ref,
-                 sig_ref, spread_ref, pack_ref, land_ref, base_ref, gain_ref, leave_ref, hop_ref, ends_ref,
+                 in_ref, sig_ref, spread_ref, pack_ref, land_ref, base_ref, gain_ref, leave_ref, hop_ref, ends_ref,
                  state_ref, left_ref, got_ref, whole_ref, wholes_ref, enter_ref, given_ref, entered_ref, first_ref,
                  long_ref, rows_ref, slide_ref, slid_ref, grad_ref, turn_ref, sums_ref,
-                 sent_ref, came_ref, final_ref, home_ref, send_sem, recv_sem, own_sem):
+                 sent_ref, came_ref, final_ref, home_ref, send_sem, recv_sem, own_sem, in_sem):
     seq, chan = lax.axis_index("seq"), lax.axis_index("chan")
     row, worker = lax.div(seq, WORKERS), lax.rem(seq, WORKERS)
+    rates_ref, weights_ref = small_ref.at[:2 * MODES], small_ref.at[2 * MODES:4 * MODES]
+    skip_ref = small_ref.at[4 * MODES:]
+    early_pair = lax.div(lax.rem(chan + 1, 4), 2)
+    pairs = (early_pair, 1 - early_pair)
+
+    for wave, pair in enumerate(pairs):
+        for group in range(GROUPS):
+            tile = 2 * group + pair
+            for at, source in enumerate((q_ref, k_ref, v_ref, o_ref)):
+                pltpu.make_async_copy(
+                    source.at[:, pl.ds(pl.multiple_of(tile * LANES, LANES), LANES)],
+                    in_ref.at[at, tile], in_sem.at[wave],
+                ).start()
+
+    def load_pair(wave):
+        settle(in_ref.at[pl.ds(0, 2)], in_sem.at[wave])
+        for group in range(GROUPS):
+            load_signals(2 * group + pairs[wave], in_ref, sig_ref)
+
     barrier = pltpu.get_barrier_semaphore()
 
     def greet(step, _):
@@ -265,13 +301,11 @@
         settle(source.at[pl.ds(0, WORKERS - 1)], send_sem.at[sem])
         settle(target.at[pl.ds(0, WORKERS - 1)], recv_sem.at[sem])
 
-    def correlate(place):
+    def prepare(place):
         own_copies[place].wait()
         settle(pack_ref.at[place, pl.ds(0, (SHARDS - 1) * 16)], send_sem.at[place])
         settle(land_ref.at[place, pl.ds(0, (SHARDS - 1) * 16)], recv_sem.at[place])
-        return correlate_filter(
-            land_ref.at[place], rows_ref, slide_ref, slid_ref, grad_ref, turn_ref, sums_ref
-        )
+        prepare_filter(land_ref.at[place], rows_ref, slide_ref, slid_ref, grad_ref, turn_ref)
 
     def share_copy(place):
         return pltpu.make_async_remote_copy(
@@ -281,30 +315,32 @@
         )
 
     def correlate_and_share(place):
-        sent_ref[place] = correlate(place).astype(BF16)
+        prepare(place)
+        parts, _ = correlate_lags(SHARDS - 1, 0, no_carry(), slid_ref, turn_ref, sums_ref)
+        sent_ref[place] = jnp.concatenate(parts, axis=0).astype(BF16)
         share_copy(place).start()
 
-    load_signals(q_ref, k_ref, v_ref, o_ref, sig_ref)
-    early_pair = lax.div(lax.rem(chan + 1, 4), 2)
+    make_decays(rates_ref, weights_ref, base_ref, gain_ref, leave_ref, hop_ref)
+    slide_ref[...] = jnp.zeros_like(slide_ref)
+    slid_ref[:, :PAD, :] = jnp.zeros_like(slid_ref[:, :PAD, :])
+
+    load_pair(0)
     pack_pair(early_pair, chan, sig_ref, spread_ref, pack_ref)
     pl.semaphore_wait(barrier, SHARDS - 1 + 3)
     send_filter(0)
 
-    make_decays(rates_ref, weights_ref, base_ref, gain_ref, leave_ref, hop_ref)
+    load_pair(1)
     block_states(sig_ref, base_ref, leave_ref, ends_ref, state_ref, left_ref)
     own_states = to_row(left_ref, got_ref, STATES)
     pack_pair(1 - early_pair, chan, sig_ref, spread_ref, pack_ref)
     send_filter(1)
-    slide_ref[...] = jnp.zeros_like(slide_ref)
-    slid_ref[:, :PAD, :] = jnp.zeros_like(slid_ref[:, :PAD, :])
 
     settle_row(left_ref, got_ref, STATES, own_states)
     tile_row = iota((TILES, LANES), 0)
-    mode_rates = rates_ref[pl.ds(worker, 1), :]
     rate = jnp.where(
         lax.rem(tile_row, 2) == 0,
-        jnp.broadcast_to(mode_rates[:, :LANES], (TILES, LANES)),
-        jnp.broadcast_to(mode_rates[:, LANES:], (TILES, LANES)),
+        jnp.broadcast_to(rates_ref[pl.ds(worker, 1), :], (TILES, LANES)),
+        jnp.broadcast_to(rates_ref[pl.ds(MODES + worker, 1), :], (TILES, LANES)),
     )
     decay = jnp.exp(-float(ROWS) * rate)
     zero = jnp.zeros((TILES, LANES), F32)
@@ -347,24 +383,31 @@
     for place in range(2 * TILES):
         first_ref[place] = state_ref[pl.ds(place, MODES, stride=2 * TILES), :]
     run_recurrence(sig_ref, base_ref, gain_ref, hop_ref, ends_ref, first_ref, long_ref)
-    finish_outputs(q_ref, k_ref, v_ref, skip_ref, sig_ref, long_ref, layer_ref, kgrad_ref, vgrad_ref)
+    finish_outputs(in_ref, skip_ref, sig_ref, long_ref, layer_ref, kgrad_ref, vgrad_ref)
 
     correlate_and_share(2)
-    taps = correlate(3)
-    for place in range(3):
-        share_copy(place).wait()
-        taps = taps + came_ref[place].astype(F32)
-    for part in range(2):
-        final_ref[:, part, :] = taps[part * SHARDS:(part + 1) * SHARDS]
-    own = pltpu.make_async_copy(final_ref.at[seq], home_ref.at[seq], own_sem.at[FINAL])
-    own.start()
-
-    def last(step, _):
-        to = lax.rem(seq + step, SHARDS)
-        seq_copy(final_ref.at[to], home_ref.at[seq], send_sem.at[FINAL], recv_sem.at[FINAL], to).start()
-        return _
-    lax.fori_loop(1, SHARDS, last, 0)
-    own.wait()
+    prepare(3)
+    carried = no_carry()
+    for upper in (1, 0):
+        low = upper * HALF
+        parts, carried = correlate_lags(low + HALF - 1, low, carried, slid_ref, turn_ref, sums_ref)
+        if upper:
+            for place in range(3):
+                share_copy(place).wait()
+        for part in range(2):
+            rows = slice(part * SHARDS + low, part * SHARDS + low + HALF)
+            shares = came_ref[0, rows, :].astype(F32) + came_ref[1, rows, :].astype(F32) + came_ref[2, rows, :].astype(F32)
+            final_ref[low:low + HALF, part, :] = parts[part] + shares
+
+        def leave(step, _):
+            to = low + lax.rem(seq + step, HALF)
+
+            @pl.when(to != seq)
+            def _send():
+                seq_copy(final_ref.at[to], home_ref.at[seq], send_sem.at[FINAL], recv_sem.at[FINAL], to).start()
+            return _
+        lax.fori_loop(0, HALF, leave, 0)
+    home_ref[seq] = final_ref[seq]
     settle(final_ref.at[pl.ds(0, SHARDS - 1)], send_sem.at[FINAL])
     settle(home_ref.at[pl.ds(0, SHARDS - 1)], recv_sem.at[FINAL])
     scale = 1.0 / math.sqrt(SEQ_LEN * (CHANNELS // FILTERS))
@@ -372,7 +415,23 @@
         taps_ref[:, part * LANES:(part + 1) * LANES] = home_ref[:, part, :] * scale
 
 
+def hand_on(*refs):
+    sources, targets, sem = refs[:4], refs[4:8], refs[8]
+    pieces = []
+    for at, source in enumerate(sources):
+        count = 4 if at < 3 else 1
+        rows = source.shape[0] // count
+        for piece in range(count):
+            some = pl.ds(piece * rows, rows)
+            pieces.append(pltpu.make_async_copy(source.at[some], targets[at].at[some], sem.at[at * 4 + piece]))
+    for copy in pieces:
+        copy.start()
+    for copy in pieces:
+        copy.wait()
+
+
 SCRATCH = [
+    pltpu.VMEM((4, TILES, ROWS, LANES), BF16),
     pltpu.VMEM((2, TILES, ROWS, LANES), F32),
     pltpu.VMEM((2, SHARDS * 16, LANES), F32),
     pltpu.VMEM((4, SHARDS * 16, LANES), BF16),
@@ -405,22 +464,37 @@
     pltpu.SemaphoreType.DMA((11,)),
     pltpu.SemaphoreType.DMA((11,)),
     pltpu.SemaphoreType.DMA((11,)),
+    pltpu.SemaphoreType.DMA((2,)),
 ]
 VMEM = pl.BlockSpec(memory_space=pltpu.VMEM)
 
 
+ANY = pl.BlockSpec(memory_space=pl.ANY)
+
+
 def per_device(query_proj, key_proj, value_proj, out_grad, residues, decay_rate, skip_gain):
     sds = jax.ShapeDtypeStruct
-    layer, kgrad, vgrad, taps = pl.pallas_call(
+    shapes = (sds((ROWS, 1024), BF16),) * 3 + (sds((SHARDS, ROWS), F32),)
+    sides = [table.T[:, side * LANES:(side + 1) * LANES] for table in (decay_rate, residues) for side in range(2)]
+    small = jnp.concatenate(sides + [skip_gain.reshape(TILES, LANES)], axis=0)
+    results = pl.pallas_call(
         layer_kernel,
-        out_shape=(sds((ROWS, 1024), BF16),) * 3 + (sds((SHARDS, ROWS), F32),),
-        in_specs=[VMEM] * 7,
+        out_shape=shapes,
+        in_specs=[ANY] * 4 + [VMEM],
         out_specs=(VMEM,) * 4,
         scratch_shapes=SCRATCH,
         compiler_params=pltpu.CompilerParams(
-            vmem_limit_bytes=56 * 2**20, collective_id=0, has_side_effects=True
+            vmem_limit_bytes=53120 * 2**10, collective_id=0, has_side_effects=True
         ),
-    )(query_proj, key_proj, value_proj, out_grad, decay_rate.T, residues.T, skip_gain[None, :])
+    )(query_proj, key_proj, value_proj, out_grad, small)
+    layer, kgrad, vgrad, taps = pl.pallas_call(
+        hand_on,
+        out_shape=shapes,
+        in_specs=[pl.BlockSpec(memory_space=pltpu.VMEM)] * 4,
+        out_specs=(pl.BlockSpec(memory_space=pltpu.HBM),) * 4,
+        scratch_shapes=[pltpu.SemaphoreType.DMA((16,))],
+        compiler_params=pltpu.CompilerParams(vmem_limit_bytes=53120 * 2**10),
+    )(*results)
     return (layer, kgrad, vgrad, taps.T)
 
 

time: 59.7 us -> 56.4 us (0.945)
  local copies, waits for them, and re-layouts: 4.65 us -> 1.44 us
    unnamed x10, local copies, waits for them, and re-layouts: 4.65 us -> 1.44 us
    pallas_call x1 -> x2, Pallas kernels: 54.2 us -> 54 us  [the longest x1 52.7 us: per_device(): pl.pallas_call(layer_kernel, out_shape=shapes, in_specs=[ANY] * 4 + [VMEM...]
where the time goes in v4:
time: 56.4 us; the launch traced here: 56.2 us
  Pallas kernels  54 us (96%)
  local copies, waits for them, and re-layouts  1.44 us (3%)
  between operations  0.84 us (1%)
    pallas_call x1, Pallas kernels, per_device(): pl.pallas_call(layer_kernel, out_shape=shapes, in_specs=[ANY] * 4 + [VMEM...  52.7 us
    unnamed x10, local copies, waits for them, and re-layouts  1.44 us
    pallas_call x1, Pallas kernels, per_device(): pl.pallas_call(hand_on, out_shape=shapes, in_specs=[pl.BlockSpec(memory_s...  1.29 us

profile of v4, /device:TPU:1, one launch (start us, length us, event | category | flops | bytes accessed | tf_op | source)
XLA Modules:
  0.0 56.2 jit_solution(16916523650616167424)
XLA Ops:
  0.6 0.0 copy-start
  0.6 0.0 copy-start.1
  0.7 0.8 %constant_dynamic-update-slice_fusion.4 = f32[72,128]{1,0:T(8,128)S(1)} fusion(f32[16,256]{1,0:T(8,128)} %bitcast.5), kind=kLoop, calls=%fused_computation.4 | loop fusion | bytes 16384
  1.4 0.0 copy-done
  1.4 0.0 copy-done.1
  1.4 0.0 copy-start.2
  1.4 0.7 %copy-done.2 = f32[1024]{0:T(1024)S(1)} copy-done((f32[1024]{0:T(1024)S(1)}, f32[1024]{0:T(1024)}, u32[]{:S(2)}) %copy-start.2) | copy-done | bytes 4120
  2.1 52.7 %shard_map.102 = (bf16[256,1024]{1,0:T(8,128)(2,1)S(1)}, bf16[256,1024]{1,0:T(8,128)(2,1)S(1)}, bf16[256,1024]{1,0:T(8,128)(2,1)S(1)}, f32[64,256]{1,0:T(8,128)S(1)}) custom-call(bf16[256,1024]{1,0:T(8,128)(2,1)} %q_ref.1, bf16[256,1024]{1,0:T(8,128)(2,1)} %k_ref.1, bf16[256,1024]{1,0:T(8,128)(2,1)} %v_ref.1, bf16[256,1024]{1,0:T(8,128)(2,1)} %o_ref.1, ...), custom_call_target="tpu_custom_call" | custom-call | tf_op jit(solution)/shard_map/pallas_call | solution.py:480
  54.8 1.3 %shard_map.103 = (bf16[256,1024]{1,0:T(8,128)(2,1)}, bf16[256,1024]{1,0:T(8,128)(2,1)}, bf16[256,1024]{1,0:T(8,128)(2,1)}, f32[64,256]{1,0:T(8,128)}) custom-call(bf16[256,1024]{1,0:T(8,128)(2,1)S(1)} %get-tuple-element.12.refs_0_, bf16[256,1024]{1,0:T(8,128)(2,1)S(1)} %get-tuple-element.13.refs_1_, bf16[256,1024]{1,0:T(8,128)(2,1)S(1)} %get-tuple-element.14.refs_2_, ...), custom_call_target="tpu_custom_call" | custom-call | tf_op jit(solution)/shard_map/pallas_call | solution.py:490
  (4 shorter events, 0.0 us)
Async XLA Ops:
  0.6 0.8 %copy-start = (f32[256,16]{0,1:T(8,128)S(1)}, f32[256,16]{0,1:T(8,128)}, u32[]{:S(2)}) copy-start(f32[256,16]{0,1:T(8,128)} %param.12) | copy-start | bytes 49156
  0.6 0.8 %copy-start.1 = (f32[256,16]{0,1:T(8,128)S(1)}, f32[256,16]{0,1:T(8,128)}, u32[]{:S(2)}) copy-start(f32[256,16]{0,1:T(8,128)} %param.11) | copy-start | bytes 49156
  1.4 0.7 %copy-start.2 = (f32[1024]{0:T(1024)S(1)}, f32[1024]{0:T(1024)}, u32[]{:S(2)}) copy-start(f32[1024]{0:T(1024)} %param.13) | copy-start | bytes 12292

commit v5 on v4

--- a/solution.py
+++ b/solution.py
@@ -65,9 +65,9 @@
 def make_decays(rates_ref, weights_ref, base_ref, gain_ref, leave_ref, hop_ref):
     sub = iota((MODES, SUBS, LANES), 1)
     for side in range(2):
-        rows = slice(side * MODES, (side + 1) * MODES)
-        rate = jnp.broadcast_to(rates_ref[rows, :][:, None, :], (MODES, SUBS, LANES))
-        weight = jnp.broadcast_to(weights_ref[rows, :][:, None, :], (MODES, SUBS, LANES))
+        lanes = slice(side * LANES, (side + 1) * LANES)
+        rate = jnp.broadcast_to(rates_ref[:, lanes][:, None, :], (MODES, SUBS, LANES))
+        weight = jnp.broadcast_to(weights_ref[:, lanes][:, None, :], (MODES, SUBS, LANES))
         base_ref[side] = jnp.exp(-rate)
         gain_ref[side] = weight * jnp.sqrt(rate)
         for sig in range(2):
@@ -142,7 +142,7 @@
 def finish_outputs(in_ref, skip_ref, sig_ref, long_ref, layer_ref, kgrad_ref, vgrad_ref):
     for tile in range(TILES):
         lanes = pl.ds(tile * LANES, LANES)
-        skip = skip_ref[tile:tile + 1, :]
+        skip = skip_ref[tile // 2:tile // 2 + 1, tile % 2 * LANES:(tile % 2 + 1) * LANES]
         layer = long_ref[0, tile] + skip * sig_ref[0, tile]
         layer_ref[:, lanes] = (in_ref[0, tile].astype(F32) * layer).astype(BF16)
         total = long_ref[1, tile] + skip * sig_ref[1, tile]
@@ -240,8 +240,7 @@
                  sent_ref, came_ref, final_ref, home_ref, send_sem, recv_sem, own_sem, in_sem):
     seq, chan = lax.axis_index("seq"), lax.axis_index("chan")
     row, worker = lax.div(seq, WORKERS), lax.rem(seq, WORKERS)
-    rates_ref, weights_ref = small_ref.at[:2 * MODES], small_ref.at[2 * MODES:4 * MODES]
-    skip_ref = small_ref.at[4 * MODES:]
+    rates_ref, weights_ref, skip_ref = small_ref.at[:MODES], small_ref.at[MODES:2 * MODES], small_ref.at[2 * MODES:]
     early_pair = lax.div(lax.rem(chan + 1, 4), 2)
     pairs = (early_pair, 1 - early_pair)
 
@@ -337,10 +336,11 @@
 
     settle_row(left_ref, got_ref, STATES, own_states)
     tile_row = iota((TILES, LANES), 0)
+    mode_rates = rates_ref[pl.ds(worker, 1), :]
     rate = jnp.where(
         lax.rem(tile_row, 2) == 0,
-        jnp.broadcast_to(rates_ref[pl.ds(worker, 1), :], (TILES, LANES)),
-        jnp.broadcast_to(rates_ref[pl.ds(MODES + worker, 1), :], (TILES, LANES)),
+        jnp.broadcast_to(mode_rates[:, :LANES], (TILES, LANES)),
+        jnp.broadcast_to(mode_rates[:, LANES:], (TILES, LANES)),
     )
     decay = jnp.exp(-float(ROWS) * rate)
     zero = jnp.zeros((TILES, LANES), F32)
@@ -374,9 +374,9 @@
     given_ref[...] = enter_ref[...].astype(BF16)
     own_entering = to_row(given_ref, entered_ref, ENTERING)
     send_filter(2)
+    send_filter(3)
 
     correlate_and_share(1)
-    send_filter(3)
 
     settle_row(given_ref, entered_ref, ENTERING, own_entering)
     state_ref[...] = entered_ref[...].astype(F32).reshape(MODES * MODES, LANES)
@@ -475,8 +475,7 @@
 def per_device(query_proj, key_proj, value_proj, out_grad, residues, decay_rate, skip_gain):
     sds = jax.ShapeDtypeStruct
     shapes = (sds((ROWS, 1024), BF16),) * 3 + (sds((SHARDS, ROWS), F32),)
-    sides = [table.T[:, side * LANES:(side + 1) * LANES] for table in (decay_rate, residues) for side in range(2)]
-    small = jnp.concatenate(sides + [skip_gain.reshape(TILES, LANES)], axis=0)
+    small = jnp.concatenate([decay_rate.T, residues.T, skip_gain.reshape(4, FILTERS)], axis=0)
     results = pl.pallas_call(
         layer_kernel,
         out_shape=shapes,

time: 56.4 us -> 56.1 us (level)
  other arithmetic: 0 us -> 0.74 us
  local copies, waits for them, and re-layouts: 1.44 us -> 0.7 us
    unnamed x10 -> x0, local copies, waits for them, and re-layouts: 1.44 us -> none
    concatenate x0 -> x1, other arithmetic: none -> 0.74 us  [per_device(): jnp.concatenate([decay_rate.T, residues.T, skip_gain.reshape(4, FILTERS)]...]
    reshape x0 -> x1, local copies, waits for them, and re-layouts: none -> 0.7 us  [per_device(): skip_gain.reshape(4, FILTERS)]
where the time goes in v5:
time: 56.1 us; the launch traced here: 55.8 us
  Pallas kernels  53.5 us (95%)
  between operations  0.8 us (1%)
  other arithmetic  0.74 us (1%)
  local copies, waits for them, and re-layouts  0.7 us (1%)
    pallas_call x1, Pallas kernels, per_device(): pl.pallas_call(layer_kernel, out_shape=shapes, in_specs=[ANY] * 4 + [VMEM...  52.3 us
    pallas_call x1, Pallas kernels, per_device(): pl.pallas_call(hand_on, out_shape=shapes, in_specs=[pl.BlockSpec(memory_s...  1.29 us

profile of v5, /device:TPU:1, one launch (start us, length us, event | category | flops | bytes accessed | tf_op | source)
XLA Modules:
  0.0 55.8 jit_solution(444439889645090118)
XLA Ops:
  0.6 0.7 %reshape.11 = f32[4,256]{1,0:T(4,128)S(1)} reshape(f32[1024]{0:T(1024)} %param.13) | data formatting | bytes 8192 | tf_op jit(solution)/shard_map/reshape | solution.py:478
  1.3 0.7 %pad_maximum_fusion.small_ref = f32[36,256]{1,0:T(8,128)S(1)} fusion(f32[4,256]{1,0:T(4,128)S(1)} %reshape.11, f32[16,256]{1,0:T(8,128)} %bitcast.3, f32[16,256]{1,0:T(8,128)} %bitcast.4), kind=kLoop, calls=%fused_computation | loop fusion | flops 18432 | bytes 73728 | tf_op jit(solution)/shard_map/concatenate | solution.py:478
  2.1 52.3 %shard_map.102 = (bf16[256,1024]{1,0:T(8,128)(2,1)S(1)}, bf16[256,1024]{1,0:T(8,128)(2,1)S(1)}, bf16[256,1024]{1,0:T(8,128)(2,1)S(1)}, f32[64,256]{1,0:T(8,128)S(1)}) custom-call(bf16[256,1024]{1,0:T(8,128)(2,1)} %q_ref.1, bf16[256,1024]{1,0:T(8,128)(2,1)} %k_ref.1, bf16[256,1024]{1,0:T(8,128)(2,1)} %v_ref.1, bf16[256,1024]{1,0:T(8,128)(2,1)} %o_ref.1, ...), custom_call_target="tpu_custom_call" | custom-call | tf_op jit(solution)/shard_map/pallas_call | solution.py:479
  54.3 1.3 %shard_map.103 = (bf16[256,1024]{1,0:T(8,128)(2,1)}, bf16[256,1024]{1,0:T(8,128)(2,1)}, bf16[256,1024]{1,0:T(8,128)(2,1)}, f32[64,256]{1,0:T(8,128)}) custom-call(bf16[256,1024]{1,0:T(8,128)(2,1)S(1)} %get-tuple-element.12.refs_0_, bf16[256,1024]{1,0:T(8,128)(2,1)S(1)} %get-tuple-element.13.refs_1_, bf16[256,1024]{1,0:T(8,128)(2,1)S(1)} %get-tuple-element.14.refs_2_, ...), custom_call_target="tpu_custom_call" | custom-call | tf_op jit(solution)/shard_map/pallas_call | solution.py:489
